TPU v7x, 32 devices: a whole 2x2x4 slice. The times are simulated.
32 devices in a mesh: group: 8 (over z, y), pencil: 4 (over x, core).
Axes of the slice: x: 2, y: 2, z: 4, core: 2. Of those that a mesh axis runs over, the one named last changes fastest.
Arguments:
- mult_iterate: float32 [8, 4, 8192], P('group', 'pencil'), may hold values from -6 to 6
- residual: float32 [8, 4, 8192], P('group', 'pencil'), may hold values from -6 to 6
- direction: float32 [8, 4, 8192], P('group', 'pencil'), may hold values from -6 to 6
- mult_scale: float32 [8, 4, 8192], P('group', 'pencil'), may hold values from 0.5 to 18
- eigen_basis: float32 [32, 3, 64, 64], P('group'), may hold values from -1 to 1
- eigen_values: float32 [32, 3, 64], P('group'), may hold values from 0.2 to 2
- elastic_coef: float32 [32, 3, 3], P('group'), may hold values from 0.5 to 2
- coarse_inverse: float32 [128, 128], replicated, may hold values from -1 to 2.5
- send_pos: int32 [8, 4, 16384], P('group', 'pencil'), may hold values from 0 to 48383, as said below
- pair_slots: int32 [8, 4, 2, 8192], P('group', 'pencil'), may hold values from 0 to 16383, as said below
- prim_rows: int32 [8, 4, 32], P('group', 'pencil'), may hold values from 0 to 16383, as said below
- coarse_idx: int32 [8, 4, 32], P('group', 'pencil'), may hold values from 0 to 127
Outputs:
- new_iterate: float32 [8, 4, 8192], P('group', 'pencil')
- new_residual: float32 [8, 4, 8192], P('group', 'pencil')
- new_direction: float32 [8, 4, 8192], P('group', 'pencil')
Inputs may be any that keep to these rules, and one draw needn't show every extreme that they name: `send_pos`: distinct within each block (g, s). `pair_slots`: in each block (g, s) the two rows together hold every number of 0 to 16383 once. `prim_rows`: distinct within each block (g, s).
All inputs are finite; a program needn't handle non-finite values.
Results may differ from a plain program's by a relative error of at most 0.0003.
Values sent between devices are 32-bit elements; how exact they have to be, the bound alone decides.
A program may use at most 128 MiB of HBM per device.

v0:
```python
import jax
import jax.numpy as jnp
from jax import lax
from jax.sharding import PartitionSpec as P


def cycle_slot(index, extent):
    cycle_size = 4 * extent - 4
    plane_index = index // cycle_size
    cycle_spot = index % cycle_size
    side_slot = jnp.where(
        cycle_spot < extent,
        cycle_spot,
        jnp.where(
            cycle_spot < 2 * extent - 2,
            cycle_spot + 1,
            jnp.where(cycle_spot < 3 * extent - 4, cycle_spot + 3, cycle_spot + 4),
        ),
    )
    return plane_index * 4 * extent + side_slot


def cycle_to_volume(cycles, extent):
    sides = cycles.reshape(cycles.shape[:-1] + (4, extent))
    count = jnp.arange(extent, dtype=jnp.int32)
    first_edge = (count == 0).astype(jnp.float32)
    last_edge = (count == extent - 1).astype(jnp.float32)
    plane = sides[..., 0, None, :] * first_edge[:, None]
    plane = plane + sides[..., 1, :, None] * first_edge[None, :]
    plane = plane + sides[..., 2, :, None] * last_edge[None, :]
    return plane + sides[..., 3, None, :] * last_edge[:, None]


def volume_to_cycle(volume):
    sides = jnp.stack(
        [volume[..., 0, :], volume[..., :, 0], volume[..., :, -1], volume[..., -1, :]], axis=-2
    )
    return sides.reshape(volume.shape[:-2] + (4 * volume.shape[-1],))


def spectrum(coeffs, along_x, along_y, along_z):
    first = coeffs[None, :, :, 0, None, None] * along_x.T[:, :, None, None, None]
    second = coeffs[None, :, :, 1, None, None] * along_y[None, :, None, :, None]
    third = coeffs[None, :, :, 2, None, None] * along_z[None, :, None, None, :]
    return first + second + third


def forward_yz(volume, basis):
    highest = lax.Precision.HIGHEST
    step_one = jnp.einsum("xpcyz,pzk->xpcyk", volume, basis[:, 2], precision=highest)
    return jnp.einsum("xpcyk,pyj->xpcjk", step_one, basis[:, 1], precision=highest)


def backward_yz(volume, basis):
    highest = lax.Precision.HIGHEST
    step_one = jnp.einsum("xpcjk,pyj->xpcyk", volume, basis[:, 1], precision=highest)
    return jnp.einsum("xpcyk,pzk->xpcyz", step_one, basis[:, 2], precision=highest)


def load_slab(arrived_rows, positions, slab_shape):
    cycle_total = slab_shape[0] * slab_shape[1] * slab_shape[2] * 4 * slab_shape[3]
    cycles = jnp.zeros((cycle_total,), jnp.float32).at[positions].set(arrived_rows)
    cycles = cycles.reshape(slab_shape[0], slab_shape[1], slab_shape[2], 4 * slab_shape[3])
    return cycle_to_volume(cycles, slab_shape[3])


def apply_inverse(arrived_rows, cycle_cells, basis, values, coeffs):
    highest = lax.Precision.HIGHEST
    pencils = lax.axis_size("pencil")
    extent = basis.shape[-1]
    patches = basis.shape[0]
    components = coeffs.shape[1]
    slab_x = extent // pencils
    slab_shape = (slab_x, patches, components, extent, extent)
    my_slab = lax.axis_index("pencil")
    row_start = my_slab * slab_x
    positions = cycle_slot(cycle_cells, extent)
    partial_yz = forward_yz(load_slab(arrived_rows, positions, slab_shape), basis)
    columns = lax.all_to_all(
        partial_yz.reshape(slab_x, patches, components, extent * extent),
        "pencil",
        split_axis=3,
        concat_axis=0,
        tiled=True,
    )
    columns = columns.reshape(extent, patches, components, slab_x, extent)
    spectral = jnp.einsum("xpcjk,pxi->ipcjk", columns, basis[:, 0], precision=highest)
    along_y = lax.dynamic_slice_in_dim(values[:, 1], row_start, slab_x, 1)
    scaled = spectral / spectrum(coeffs, values[:, 0], along_y, values[:, 2])
    mixed = jnp.einsum("ipcjk,pxi->xpcjk", scaled, basis[:, 0], precision=highest)
    mixed = mixed.reshape(extent, patches, components, slab_x * extent)
    back_x = lax.all_to_all(mixed, "pencil", split_axis=0, concat_axis=3, tiled=True).reshape(
        slab_shape
    )
    displace = backward_yz(back_x, basis)
    return volume_to_cycle(displace).reshape(-1)[positions]


def body(
    mult_iterate,
    residual,
    direction,
    mult_scale,
    eigen_basis,
    eigen_values,
    elastic_coef,
    coarse_inverse,
    send_pos,
    pair_slots,
    prim_rows,
    coarse_idx,
):
    highest = lax.Precision.HIGHEST
    groups = lax.axis_size("group")
    iterate_now = mult_iterate[0, 0]
    resid_now = residual[0, 0]
    search_dir = direction[0, 0]
    scale_now = mult_scale[0, 0]
    pair_rows = pair_slots[0, 0]
    cycle_cells = send_pos[0, 0]
    primal = prim_rows[0, 0]
    coarse_ids = coarse_idx[0, 0]
    rows_count = cycle_cells.shape[0]
    per_owner = rows_count // groups
    coarse_count = coarse_inverse.shape[0]
    old_part = jnp.sum(resid_now * scale_now * resid_now)
    old_norm = lax.psum(old_part, ("group", "pencil"))
    back_rows = (
        jnp.zeros((rows_count,), jnp.float32)
        .at[pair_rows[0]]
        .set(search_dir)
        .at[pair_rows[1]]
        .set(-search_dir)
    )
    arrived_rows = lax.all_to_all(
        back_rows.reshape(groups, per_owner), "group", split_axis=0, concat_axis=0, tiled=True
    ).reshape(rows_count)
    picked = apply_inverse(arrived_rows, cycle_cells, eigen_basis, eigen_values, elastic_coef)
    onehot = (coarse_ids[:, None] == jnp.arange(coarse_count, dtype=jnp.int32)[None, :]).astype(
        jnp.float32
    )
    local_coarse = jnp.dot(picked[primal], onehot, precision=highest)
    total_coarse = lax.psum(local_coarse, ("group", "pencil"))
    lifted = jnp.dot(coarse_inverse, total_coarse, precision=highest)
    sent_rows = picked.at[primal].add(jnp.dot(onehot, lifted, precision=highest))
    owner_rows = lax.all_to_all(
        sent_rows.reshape(groups, per_owner), "group", split_axis=0, concat_axis=0, tiled=True
    ).reshape(rows_count)
    mapped = owner_rows[pair_rows[0]] - owner_rows[pair_rows[1]]
    curvature = lax.psum(jnp.sum(search_dir * mapped), ("group", "pencil"))
    step_size = old_norm / curvature
    iterate_next = iterate_now + step_size * search_dir
    resid_next = resid_now - step_size * mapped
    precond = scale_now * resid_next
    norm_next = lax.psum(jnp.sum(resid_next * precond), ("group", "pencil"))
    search_next = precond + norm_next / old_norm * search_dir
    return (iterate_next[None, None], resid_next[None, None], search_next[None, None])


def solution(mesh):
    in_specs = (
        P("group", "pencil", None),
        P("group", "pencil", None),
        P("group", "pencil", None),
        P("group", "pencil", None),
        P("group", None, None, None),
        P("group", None, None),
        P("group", None, None),
        P(),
        P("group", "pencil", None),
        P("group", "pencil", None, None),
        P("group", "pencil", None),
        P("group", "pencil", None),
    )
    out_specs = (P("group", "pencil", None), P("group", "pencil", None), P("group", "pencil", None))
    return jax.shard_map(body, mesh=mesh, in_specs=in_specs, out_specs=out_specs, check_vma=False)
```

profile of v0, /device:TPU:0, one launch (start us, length us, event | category | flops | bytes accessed | tf_op | source)
XLA Modules:
  0.0 833.4 jit_solution(1552345182610651184)
XLA Ops:
  0.6 1.0 compare_select_fusion.4
  1.6 0.8 neg.3
  2.4 31.2 %scatter_custom_fusion = f32[16384]{0:T(1024)} fusion(s32[8192]{0:T(1024)S(1)} %bitcast.162, f32[8192]{0:T(1024)} %bitcast.154, f32[]{:T(128)} %constant.16.clone.1), kind=kCustom, calls=%fused_computation.78 | custom fusion | bytes 66048 | tf_op jit(solution)/shard_map/scatter | solution.py:131
  33.6 31.9 %scatter_fusion = f32[16384]{0:T(1024)} fusion(f32[16384]{0:T(1024)} %scatter_custom_fusion, s32[8192]{0:T(1024)S(1)} %bitcast.151, f32[8192]{0:T(1024)S(1)} %neg.3), kind=kCustom, calls=%fused_computation.5 | custom fusion | bytes 131072 | tf_op jit(solution)/shard_map/scatter | solution.py:133
  65.6 7.3 all-to-all-start
  72.8 0.8 compare_select_fusion
  73.6 6.1 all-to-all-done
  79.7 60.9 %scatter_custom_fusion.2 = f32[49152]{0:T(1024)S(1)} fusion(s32[16384]{0:T(1024)S(1)} %bitcast.160, f32[16384]{0:T(1024)S(1)} %bitcast.165, f32[]{:T(128)} %constant.16.clone.1), kind=kCustom, calls=%fused_computation.67 | custom fusion | bytes 196612 | tf_op jit(solution)/shard_map/scatter | solution.py:62
  140.7 0.2 reshape_reshape.6
  140.9 0.3 fusion.59
  141.5 8.2 fusion.8
  149.7 12.2 %fusion.26 = f32[16,4,3,64,64]{3,4,2,0,1:T(8,128)} fusion(f32[4,16,3,64,64]{4,3,2,1,0:T(8,128)S(1)} %fusion.8, f32[4,3,64,64]{3,2,1,0:T(8,128)S(1)} %copy-done.2), kind=kOutput, calls=%fused_computation.35 | convolution fusion | flops 603979776 | bytes 9568256 | tf_op jit(solution)/shard_map/xpcyk,pyj->xpcjk/dot_general | solution.py:51
  161.9 25.9 %copy.135 = f32[16,4,3,64,64]{0,1,2,4,3:T(4,128)} copy(f32[16,4,3,64,64]{3,4,2,0,1:T(8,128)} %fusion.26) | data formatting | bytes 6291456 | tf_op jit(solution)/shard_map/reshape | solution.py:80
  187.8 33.3 %reshape.387 = f32[4,1,196608]{2,1,0:T(1,128)} reshape(f32[4096,3,4,16]{3,2,1,0:T(4,128)} %bitcast.146) | data formatting | bytes 6291456
  221.1 3.8 all-to-all-start.1
  224.9 0.1 fusion.60
  225.0 0.1 copy.117
  225.1 0.1 copy.116
  225.2 0.1 copy.118
  225.3 0.1 dynamic-slice_bitcast_fusion
  225.4 0.1 broadcast_multiply_fusion.2
  225.6 0.1 broadcast_add_fusion
  225.7 36.1 %all-to-all-done.1 = f32[4,1,196608]{2,1,0:T(1,128)S(1)} async-done(((f32[4,1,196608]{2,1,0:T(1,128)}), f32[4,1,196608]{2,1,0:T(1,128)S(1)}, u32[]{:S(2)}, u32[]{:S(2)}) %all-to-all-start.1) | async-done | bytes 3145760 | tf_op jit(solution)/shard_map/all_to_all | solution.py:79
  261.8 1.6 copy-done.1
  263.4 0.5 broadcast.300
  263.9 10.4 %reduce = f32[4,196608]{1,0:T(4,128)S(1)} reduce(f32[4,1,196608]{2,1,0:T(1,128)} %copy-done.1, f32[]{:T(128)} %broadcast.300), dimensions={1}, to_apply=%all_to_all.36.reduce_sub_computation | reduce | bytes 6291460 | tf_op jit(solution)/shard_map/all_to_all | solution.py:79
  274.3 28.0 %reshape.388 = f32[4096,3,4,16]{3,2,1,0:T(4,128)} reshape(f32[4,196608]{1,0:T(4,128)S(1)} %reduce) | data formatting | bytes 6291456
  302.3 19.5 %copy.113 = f32[4,16,4,3,1024]{4,1,0,3,2:T(8,128)S(1)} copy(f32[4,16,4,3,1024]{1,2,3,4,0:T(4,128)} %bitcast.145) | data formatting | bytes 6291456 | tf_op jit(solution)/shard_map/all_to_all | solution.py:79
  321.8 3.7 reshape.305
  325.5 14.1 %fusion.5 = f32[4,3,16,64,64]{4,3,2,1,0:T(8,128)S(1)} fusion(f32[64,4,3,16,64]{4,3,0,2,1:T(8,128)} %reshape.305, f32[4,3,64,64]{3,2,1,0:T(8,128)} %param.16), kind=kOutput, calls=%fused_computation.14 | convolution fusion | flops 603979776 | bytes 9568256 | tf_op jit(solution)/shard_map/xpcjk,pxi->ipcjk/dot_general | solution.py:87
  339.7 8.9 %fusion.2 = f32[4,3,16,64,64]{4,3,2,1,0:T(8,128)} fusion(f32[4,3,16,64,64]{4,3,2,1,0:T(8,128)S(1)} %fusion.5, f32[4,3,64]{2,1,0:T(4,128)S(1)} %broadcast_multiply_fusion.1, f32[64,4,3,16]{0,3,2,1:T(8,128)S(1)} %broadcast_add_fusion, f32[4,3,64,64]{3,2,1,0:T(8,128)} %param.16), kind=kOutput, calls=%fused_computation.11 | convolution fusion | flops 605552640 | bytes 6474752 | tf_op jit(solution)/shard_map/ipcjk,pxi->xpcjk/dot_general | solution.py:90
  348.6 5.9 copy.119
  354.5 4.1 all-to-all-start.2
  358.7 36.8 %all-to-all-done.2 = f32[64,4,3,1024]{3,1,2,0:T(4,128)S(1)} async-done(((f32[64,4,3,1024]{3,1,2,0:T(4,128)}), f32[64,4,3,1024]{3,1,2,0:T(4,128)S(1)}, u32[]{:S(2)}, u32[]{:S(2)}) %all-to-all-start.2) | async-done | bytes 3145760 | tf_op jit(solution)/shard_map/all_to_all | solution.py:92
  395.5 1.8 copy.120
  397.3 2.0 copy.140
  399.3 4.3 reshape.382
  403.6 12.4 %fusion.35 = f32[4,16,3,64,64]{4,3,2,1,0:T(8,128)S(1)} fusion(f32[16,4,3,64,64]{4,3,2,0,1:T(8,128)} %reshape.382, f32[4,3,64,64]{3,2,1,0:T(8,128)} %param.16), kind=kOutput, calls=%fused_computation.52 | convolution fusion | flops 603979776 | bytes 9568256 | tf_op jit(solution)/shard_map/xpcjk,pyj->xpcyk/dot_general | solution.py:56
  416.0 10.8 %fusion.29 = f32[16,4,3,64,64]{4,3,2,0,1:T(8,128)S(1)} fusion(f32[4,16,3,64,64]{4,3,2,1,0:T(8,128)S(1)} %fusion.35, f32[4,3,64,64]{3,2,1,0:T(8,128)} %param.16), kind=kOutput, calls=%fused_computation.36 | convolution fusion | flops 603979776 | bytes 6422528 | tf_op jit(solution)/shard_map/xpcyk,pzk->xpcyz/dot_general | solution.py:57
  426.8 6.9 fusion.58
  433.7 0.1 fusion.57
  433.9 4.6 copy.124
  438.4 0.1 copy.126
  438.6 4.6 copy.125
  443.1 0.1 copy.127
  443.3 0.5 pad_maximum_fusion
  443.8 0.2 reshape_reshape.7
  444.1 160.3 %gather_fusion = f32[16384]{0:T(1024)} fusion(f32[49152]{0:T(1024)S(1)} %reshape_reshape.7, s32[16384]{0:T(1024)S(1)} %broadcast_clamp_fusion), kind=kCustom, calls=%fused_computation | custom fusion | bytes 196608 | tf_op jit(solution)/shard_map/gather | solution.py:96
  604.4 1.5 gather_fusion.1
  605.9 0.2 convolution_bitcast_fusion.2
  606.1 37.9 %psum.29 = f32[128]{0:T(128)S(1)} all-reduce(f32[128]{0:T(128)S(1)} %convolution_bitcast_fusion.2), channel_id=1, replica_groups=mesh['group'=8,'pencil'=4] {'group','pencil'}, use_global_device_ids=true, to_apply=%region_5.6 | all-reduce | flops 128 | bytes 1024 | tf_op jit(solution)/shard_map/psum | solution.py:143
  644.0 0.2 convolution_bitcast_fusion.1
  644.2 0.2 convolution_bitcast_fusion
  644.4 2.2 scatter_fusion.1
  646.6 4.9 all-to-all-start.3
  651.5 0.6 fusion.48
  652.1 6.3 all-to-all-done.3
  658.4 45.5 %gather_fusion.3 = f32[8192]{0:T(1024)S(1)} fusion(f32[16384]{0:T(1024)S(1)} %bitcast.143, s32[8192]{0:T(1024)S(1)} %broadcast_clamp_fusion.1), kind=kCustom, calls=%fused_computation.3 | custom fusion | bytes 98304 | tf_op jit(solution)/shard_map/gather | solution.py:149
  704.0 45.5 %gather_fusion.2 = f32[8192]{0:T(1024)S(1)} fusion(f32[16384]{0:T(1024)S(1)} %bitcast.144, s32[8192]{0:T(1024)S(1)} %broadcast_clamp_fusion.2), kind=kCustom, calls=%fused_computation.2 | custom fusion | bytes 98304 | tf_op jit(solution)/shard_map/gather | solution.py:149
  749.5 0.6 multiply_reduce_fusion
  750.1 38.2 %all-reduce = (f32[]{:T(128)}, f32[]{:T(128)}) all-reduce(f32[]{:T(128)} %fusion.48, f32[]{:T(128)} %get-tuple-element.9), channel_id=1, replica_groups=mesh['group'=8,'pencil'=4] {'group','pencil'}, use_global_device_ids=true, to_apply=%region_1.0 | all-reduce | flops 2 | bytes 16 | tf_op jit(solution)/shard_map/psum | solution.py:127
  789.6 0.6 fusion.49
  790.2 40.9 %psum.31 = f32[]{:T(128)} all-reduce(f32[]{:T(128)} %get-tuple-element.7), channel_id=1, replica_groups=mesh['group'=8,'pencil'=4] {'group','pencil'}, use_global_device_ids=true, to_apply=%region_10.11 | all-reduce | flops 1 | bytes 8 | tf_op jit(solution)/shard_map/psum | solution.py:155
  832.5 0.7 multiply_add_fusion
  (39 shorter events, 0.5 us)
Async XLA Ops:
  0.6 643.4 %copy-start = (f32[128,128]{1,0:T(8,128)S(1)}, f32[128,128]{1,0:T(8,128)}, u32[]{:S(2)}) copy-start(f32[128,128]{1,0:T(8,128)} %param.19) | copy-start | bytes 196612
  33.6 39.2 %copy-start.6 = (s32[1,1,16384]{2,1,0:T(1,128)S(1)}, s32[1,1,16384]{2,1,0:T(1,128)}, u32[]{:S(2)}) copy-start(s32[1,1,16384]{2,1,0:T(1,128)} %param.20) | copy-start | bytes 196612
  33.6 107.8 %copy-start.2 = (f32[4,3,64,64]{3,2,1,0:T(8,128)S(1)}, f32[4,3,64,64]{3,2,1,0:T(8,128)}, u32[]{:S(2)}) copy-start(f32[4,3,64,64]{3,2,1,0:T(8,128)} %param.16) | copy-start | bytes 589828
  65.6 14.2 %all-to-all-start = ((f32[8,1,2048]{2,1,0:T(1,128)}), f32[8,1,2048]{2,1,0:T(1,128)S(1)}, u32[]{:S(2)}, u32[]{:S(2)}) async-start(f32[8,1,2048]{2,1,0:T(1,128)} %bitcast.11), calls=%async_computation | async-start | bytes 131072 | tf_op jit(solution)/shard_map/all_to_all | solution.py:135
  221.0 3.8 copy-start.7
  221.0 4.3 copy-start.9
  221.1 40.7 %all-to-all-start.1 = ((f32[4,1,196608]{2,1,0:T(1,128)}), f32[4,1,196608]{2,1,0:T(1,128)S(1)}, u32[]{:S(2)}, u32[]{:S(2)}) async-start(f32[4,1,196608]{2,1,0:T(1,128)} %reshape.387), calls=%async_computation.1 | async-start | bytes 6291456 | tf_op jit(solution)/shard_map/all_to_all | solution.py:79
  261.8 1.6 copy-start.1
  348.6 10.0 %copy-start.10 = (s32[1,1,32]{2,1,0:T(1,128)S(1)}, s32[1,1,32]{2,1,0:T(1,128)}, u32[]{:S(2)}) copy-start(s32[1,1,32]{2,1,0:T(1,128)} %param.22) | copy-start | bytes 388
  354.5 41.0 %all-to-all-start.2 = ((f32[64,4,3,1024]{3,1,2,0:T(4,128)}), f32[64,4,3,1024]{3,1,2,0:T(4,128)S(1)}, u32[]{:S(2)}, u32[]{:S(2)}) async-start(f32[64,4,3,1024]{3,1,2,0:T(4,128)} %copy.119), calls=%async_computation.2 | async-start | bytes 6291456 | tf_op jit(solution)/shard_map/all_to_all | solution.py:92
  444.0 161.9 %copy-start.11 = (s32[1,1,32]{2,1,0:T(1,128)S(1)}, s32[1,1,32]{2,1,0:T(1,128)}, u32[]{:S(2)}) copy-start(s32[1,1,32]{2,1,0:T(1,128)} %param.23) | copy-start | bytes 388
  444.0 207.5 %copy-start.4 = (f32[1,1,8192]{2,1,0:T(1,128)S(1)}, f32[1,1,8192]{2,1,0:T(1,128)}, u32[]{:S(2)}) copy-start(f32[1,1,8192]{2,1,0:T(1,128)} %param.15) | copy-start | bytes 98308
  444.0 207.5 %copy-start.5 = (f32[1,1,8192]{2,1,0:T(1,128)S(1)}, f32[1,1,8192]{2,1,0:T(1,128)}, u32[]{:S(2)}) copy-start(f32[1,1,8192]{2,1,0:T(1,128)} %param.13) | copy-start | bytes 98308
  646.6 11.8 %all-to-all-start.3 = ((f32[8,1,2048]{2,1,0:T(1,128)}), f32[8,1,2048]{2,1,0:T(1,128)S(1)}, u32[]{:S(2)}, u32[]{:S(2)}) async-start(f32[8,1,2048]{2,1,0:T(1,128)} %bitcast.57), calls=%async_computation.3 | async-start | bytes 131072 | tf_op jit(solution)/shard_map/all_to_all | solution.py:146
  703.9 45.6 %copy-start.3 = (f32[1,1,8192]{2,1,0:T(1,128)S(1)}, f32[1,1,8192]{2,1,0:T(1,128)}, u32[]{:S(2)}) copy-start(f32[1,1,8192]{2,1,0:T(1,128)} %param.14) | copy-start | bytes 98308
  704.0 128.5 %copy-start.8 = (f32[1,1,8192]{2,1,0:T(1,128)S(1)}, f32[1,1,8192]{2,1,0:T(1,128)}, u32[]{:S(2)}) copy-start(f32[1,1,8192]{2,1,0:T(1,128)} %param.12) | copy-start | bytes 98308
where the time goes:
time: 839 us; the launch traced here: 833 us
  local copies, waits for them, and re-layouts  521 us (62%)
  blocking collectives  117 us (14%)
  waiting for transfers between devices  85.3 us (10%)
  matrix products  67.3 us (8%)
  starting transfers between devices  20.1 us (2%)
  other arithmetic  18.5 us (2%)
    gather x1, local copies, waits for them, and re-layouts, apply_inverse(): return volume_to_cycle(displace).reshape(-1)[positions]  160 us
    gather x2, local copies, waits for them, and re-layouts, body(): mapped = owner_rows[pair_rows[0]] - owner_rows[pair_rows[1]]  91.1 us
    scatter x2, local copies, waits for them, and re-layouts, body(): back_rows = jnp.zeros((rows_count,), jnp.float32).at[pair_rows[0]].set(se...  63.1 us
    unnamed x26, local copies, waits for them, and re-layouts  63 us
    scatter x1, local copies, waits for them, and re-layouts, load_slab(): jnp.zeros((cycle_total,), jnp.float32).at[positions].set(arrived_rows)  60.9 us
    psum x1, blocking collectives, body(): norm_next = lax.psum(jnp.sum(resid_next * precond), ('group', 'pencil'))  40.9 us
    psum x1, blocking collectives, body(): old_norm = lax.psum(old_part, ('group', 'pencil'))  38.2 us
    psum x1, blocking collectives, body(): total_coarse = lax.psum(local_coarse, ('group', 'pencil'))  37.9 us
  transfers between devices with their start and end apart: 4, of which 4 were waited for; matrix products, arithmetic and copies ran while one was open for 0% of the time, Pallas kernels for 0%

commit v1 on v0

v1 whole, which is shorter than its diff:
```python
import functools

import jax
import jax.numpy as jnp
from jax import lax
from jax.experimental import pallas as pl
from jax.experimental.pallas import tpu as pltpu
from jax.sharding import PartitionSpec as P

LANES = 128
F32 = jnp.float32
BF16 = jnp.bfloat16
HIGHEST = lax.Precision.HIGHEST
MESH = pl.DeviceIdType.MESH
NT = (((1,), (1,)), ((), ()))
NN = (((1,), (0,)), ((), ()))


def exact_dot(left, right, dims=NN):
    return lax.dot_general(left, right, dims, precision=HIGHEST, preferred_element_type=F32)


def fast_dot(left, right, dims=NN):
    return lax.dot_general(left, right, dims, preferred_element_type=F32)


def halves(values):
    top = values.astype(BF16).astype(F32)
    return top, values - top


def floor_div(values, divisor):
    return ((values.astype(F32) + 0.5) * (1.0 / divisor)).astype(jnp.int32)


def iota(shape, dim):
    return lax.broadcasted_iota(jnp.int32, shape, dim)


def column(row):
    size = row.shape[1]
    diagonal = iota((size, size), 0) == iota((size, size), 1)
    return jnp.sum(jnp.where(diagonal, row, 0.0), axis=1, keepdims=True)


def one_hot(rows, count):
    return jnp.where(iota((count, rows.shape[1]), 0) == rows, 1.0, 0.0).astype(BF16)


def block_diagonal(blocks):
    total = sum(block.shape[1] for block in blocks)
    rows, before = [], 0
    for block in blocks:
        height, width = block.shape
        parts = [block]
        if before:
            parts = [jnp.zeros((height, before), F32)] + parts
        if total - before - width:
            parts = parts + [jnp.zeros((height, total - before - width), F32)]
        rows.append(jnp.concatenate(parts, axis=1) if len(parts) > 1 else block)
        before += width
    return jnp.concatenate(rows, axis=0)


def kernel(
    groups,
    pencils,
    iterate_ref,
    resid_ref,
    dir_ref,
    scale_ref,
    basis_ref,
    values_ref,
    coef_ref,
    inverse_ref,
    pos_ref,
    pair_ref,
    prim_ref,
    cidx_ref,
    iterate_out,
    resid_out,
    dir_out,
    back_acc,
    back_send,
    rows_in,
    row_of,
    slot_of,
    load_acc,
    load_send,
    load_in,
    diag_t,
    diag,
    diag_x,
    fwd,
    y_first,
    y_last,
    y_weight,
    bwd,
    out_send,
    out_in,
    table,
    picked,
    coarse_send,
    coarse_in,
    coarse_send2,
    coarse_in2,
    owner_in,
    image,
    sums_send,
    sums_in,
    sums_send2,
    sums_in2,
    a_send,
    a_recv,
    b_send,
    b_recv,
    c_send,
    c_recv,
    d_send,
    d_recv,
    d2_send,
    d2_recv,
    e_send,
    e_recv,
    f_send,
    f_recv,
    f2_send,
    f2_recv,
):
    group = lax.axis_index("group")
    pencil = lax.axis_index("pencil")
    patches, _, extent, _ = basis_ref.shape
    comps = coef_ref.shape[1]
    slab = extent // pencils
    share_rows = pos_ref.shape[1]
    row_blocks = groups * share_rows
    mult_rows = dir_ref.shape[0]
    slots = 4 * extent
    dup = pencils // patches
    local_i = extent // dup
    width = comps * local_i
    chunk = slab * comps
    table_rows = patches * chunk
    patch = pencil // dup
    part = lax.rem(pencil, dup)

    def group_peer(offset):
        return lax.rem(group + offset, groups)

    def pencil_peer(offset):
        return lax.rem(pencil + offset, pencils)

    def send_group(src_of, landing, send, recv):
        copies = []
        for offset in range(1, groups):
            peer = group_peer(offset)
            copy = pltpu.make_async_remote_copy(
                src_ref=src_of(peer),
                dst_ref=landing.at[group],
                send_sem=send.at[offset],
                recv_sem=recv.at[offset],
                device_id=(peer, pencil),
                device_id_type=MESH,
            )
            copy.start()
            copies.append(copy)
        return copies

    def send_pencil(src_of, landing, send, recv):
        copies = []
        for offset in range(1, pencils):
            peer = pencil_peer(offset)
            copy = pltpu.make_async_remote_copy(
                src_ref=src_of(peer),
                dst_ref=landing.at[pencil],
                send_sem=send.at[offset],
                recv_sem=recv.at[offset],
                device_id=(group, peer),
                device_id_type=MESH,
            )
            copy.start()
            copies.append(copy)
        return copies

    def finish(copies):
        for copy in copies:
            copy.wait_recv()
        for copy in copies:
            copy.wait_send()

    barrier = pltpu.get_barrier_semaphore()
    for offset in range(1, groups):
        pl.semaphore_signal(
            barrier, inc=1, device_id=(group_peer(offset), pencil), device_id_type=MESH
        )
    for offset in range(1, pencils):
        pl.semaphore_signal(
            barrier, inc=1, device_id=(group, pencil_peer(offset)), device_id_type=MESH
        )

    back_acc[...] = jnp.zeros_like(back_acc)

    def back_step(block, carry):
        base = pl.multiple_of(block * 8, 8)
        lane_base = pl.multiple_of(block * 8 * LANES, 8 * LANES)
        values = dir_ref[pl.ds(base, 8), :]
        pairs = pair_ref[:, pl.ds(lane_base, 8 * LANES)]
        high = lax.shift_right_logical(pairs, 7)
        low = jnp.bitwise_and(pairs, LANES - 1)
        tops, rests = halves(values)
        left, right = [], []
        for i in range(8):
            lanes = slice(i * LANES, (i + 1) * LANES)
            for side, sign in ((0, 1.0), (1, -1.0)):
                here = iota((row_blocks, LANES), 0) == high[side : side + 1, lanes]
                left.append(
                    jnp.concatenate(
                        [
                            jnp.where(here, sign * tops[i : i + 1], 0.0).astype(BF16),
                            jnp.where(here, sign * rests[i : i + 1], 0.0).astype(BF16),
                        ],
                        axis=0,
                    )
                )
                right.append(one_hot(low[side : side + 1, lanes], LANES))
        back_acc[...] += fast_dot(
            jnp.concatenate(left, axis=1), jnp.concatenate(right, axis=1), NT
        )
        return carry

    lax.fori_loop(0, mult_rows // 8, back_step, 0)
    for h in range(groups):
        rows = slice(h * share_rows, (h + 1) * share_rows)
        low_rows = slice(row_blocks + h * share_rows, row_blocks + (h + 1) * share_rows)
        back_send[h] = back_acc[rows, :] + back_acc[low_rows, :]

    pl.semaphore_wait(barrier, groups + pencils - 2)
    copies_a = send_group(lambda peer: back_send.at[peer], rows_in, a_send, a_recv)
    rows_in[group] = back_send[group]

    cells = pos_ref[...]
    cycle = 4 * extent - 4
    plane = floor_div(cells, cycle)
    spot = cells - plane * cycle
    slot_of[...] = (
        spot
        + jnp.where(spot >= extent, 1, 0)
        + jnp.where(spot >= 2 * extent - 2, 2, 0)
        + jnp.where(spot >= 3 * extent - 4, 1, 0)
    )
    x_index = floor_div(plane, patches * comps)
    rest = plane - x_index * (patches * comps)
    p_index = floor_div(rest, comps)
    c_index = rest - p_index * comps
    row_of[...] = p_index * chunk + c_index * slab + x_index

    basis_x = basis_ref[patch, 0]
    basis_y = basis_ref[patch, 1]
    basis_z = basis_ref[patch, 2]
    spectrum = values_ref[patch]
    along_x = spectrum[0:1]
    if dup > 1:
        basis_x = sum(
            jnp.where(part == u, basis_x[:, u * local_i : (u + 1) * local_i], 0.0)
            for u in range(dup)
        )
        along_x = sum(
            jnp.where(part == u, along_x[:, u * local_i : (u + 1) * local_i], 0.0)
            for u in range(dup)
        )
    diag[...] = block_diagonal([basis_z, basis_y, basis_y, basis_z])
    basis_yt, basis_zt = basis_y.T, basis_z.T
    diag_t[...] = block_diagonal([basis_zt, basis_yt, basis_yt, basis_zt])
    diag_x[...] = block_diagonal([basis_x] * comps)
    coef = coef_ref[patch]
    ones = jnp.ones((1, local_i), F32)
    weight_x = jnp.concatenate([coef[c : c + 1, 0:1] * along_x for c in range(comps)], axis=1)
    weight_y = jnp.concatenate([coef[c : c + 1, 1:2] * ones for c in range(comps)], axis=1)
    weight_z = jnp.concatenate([coef[c : c + 1, 2:3] * ones for c in range(comps)], axis=1)
    y_weight[...] = column(spectrum[1:2]) * weight_y
    wide = jnp.ones((1, width), F32)
    y_first[...] = column(basis_y[0:1]) * wide
    y_last[...] = column(basis_y[extent - 1 : extent]) * wide
    xz_weight = weight_x + column(spectrum[2:3]) * weight_z
    z_first = column(basis_z[0:1]) * wide
    z_last = column(basis_z[extent - 1 : extent]) * wide
    load_acc[...] = jnp.zeros_like(load_acc)
    finish(copies_a)

    def load_step(h, carry):
        values = rows_in[h]
        rows, columns = row_of[h], slot_of[h]
        tops, rests = halves(values)
        left, right = [], []
        for i in range(share_rows):
            here = iota((table_rows, LANES), 0) == rows[i : i + 1]
            left.append(
                jnp.concatenate(
                    [
                        jnp.where(here, tops[i : i + 1], 0.0).astype(BF16),
                        jnp.where(here, rests[i : i + 1], 0.0).astype(BF16),
                    ],
                    axis=0,
                )
            )
            right.append(one_hot(columns[i : i + 1], slots))
        load_acc[...] += fast_dot(
            jnp.concatenate(left, axis=1), jnp.concatenate(right, axis=1), NT
        )
        return carry

    lax.fori_loop(0, groups, load_step, 0)
    for p in range(patches):
        load_send[p] = (
            load_acc[p * chunk : (p + 1) * chunk, :]
            + load_acc[table_rows + p * chunk : table_rows + (p + 1) * chunk, :]
        )
    copies_b = send_pencil(lambda peer: load_send.at[peer // dup], load_in, b_send, b_recv)
    load_in[pencil] = load_send[patch]
    finish(copies_b)

    sides = jnp.concatenate(
        [load_in[s, c * slab : (c + 1) * slab, :] for c in range(comps) for s in range(pencils)],
        axis=0,
    )
    fwd[...] = exact_dot(exact_dot(diag_t[...], sides, NT), diag_x[...])
    side_a = fwd[0:extent, :]
    side_d = fwd[3 * extent : 4 * extent, :]

    def solve_step(block, carry):
        sum_first, sum_last = carry
        base = pl.multiple_of(block * 8, 8)
        first = y_first[pl.ds(base, 8), :]
        last = y_last[pl.ds(base, 8), :]
        weight = y_weight[pl.ds(base, 8), :]
        side_b = fwd[pl.ds(extent + base, 8), :]
        side_c = fwd[pl.ds(2 * extent + base, 8), :]
        out_b, out_c = [], []
        for i in range(8):
            row = slice(i, i + 1)
            spectral = (
                first[row] * side_a + last[row] * side_d + side_b[row] * z_first + side_c[row] * z_last
            )
            scaled = spectral / (xz_weight + weight[row])
            sum_first = sum_first + first[row] * scaled
            sum_last = sum_last + last[row] * scaled
            out_b.append(jnp.sum(z_first * scaled, axis=0, keepdims=True))
            out_c.append(jnp.sum(z_last * scaled, axis=0, keepdims=True))
        bwd[pl.ds(extent + base, 8), :] = jnp.concatenate(out_b, axis=0)
        bwd[pl.ds(2 * extent + base, 8), :] = jnp.concatenate(out_c, axis=0)
        return sum_first, sum_last

    zero = jnp.zeros((extent, width), F32)
    sum_first, sum_last = lax.fori_loop(0, extent // 8, solve_step, (zero, zero))
    bwd[0:extent, :] = sum_first
    bwd[3 * extent : 4 * extent, :] = sum_last
    cells_out = exact_dot(diag_x[...], exact_dot(diag[...], bwd[...]), NT)
    for s in range(pencils):
        out_send[s] = jnp.concatenate(
            [
                cells_out[c * extent + s * slab : c * extent + (s + 1) * slab, :]
                for c in range(comps)
            ],
            axis=0,
        )
    copies_c = send_pencil(lambda peer: out_send.at[peer], out_in, c_send, c_recv)
    out_in[pencil] = out_send[pencil]
    finish(copies_c)

    for p in range(patches):
        total = out_in[p * dup]
        for u in range(1, dup):
            total = total + out_in[p * dup + u]
        top, rest_part = halves(total)
        table[p * chunk : (p + 1) * chunk, :] = top
        table[table_rows + p * chunk : table_rows + (p + 1) * chunk, :] = rest_part
    lookup = table[...].astype(BF16)

    def pick_step(h, carry):
        rows, columns = row_of[h], slot_of[h]
        found = []
        for i in range(0, share_rows, 2):
            hot = jnp.concatenate(
                [one_hot(columns[i : i + 1], slots), one_hot(columns[i + 1 : i + 2], slots)], axis=1
            )
            both = fast_dot(lookup, hot)
            both = both[0:table_rows] + both[table_rows : 2 * table_rows]
            for u in range(2):
                here = iota((table_rows, LANES), 0) == rows[i + u : i + u + 1]
                found.append(
                    jnp.sum(
                        jnp.where(here, both[:, u * LANES : (u + 1) * LANES], 0.0),
                        axis=0,
                        keepdims=True,
                    )
                )
        picked[h] = jnp.concatenate(found, axis=0)
        return carry

    lax.fori_loop(0, groups, pick_step, 0)

    primal = prim_ref[...]
    count = primal.shape[1]
    prim_high = lax.shift_right_logical(primal, 7)
    prim_low = jnp.bitwise_and(primal, LANES - 1)
    hot_high = jnp.where(iota((row_blocks, count), 0) == prim_high, 1.0, 0.0)
    hot_low = jnp.where(iota((LANES, count), 0) == prim_low, 1.0, 0.0)
    coarse_count = inverse_ref.shape[0]
    hot_coarse = jnp.where(iota((coarse_count, count), 0) == cidx_ref[...], 1.0, 0.0)
    flat = jnp.concatenate([picked[h] for h in range(groups)], axis=0)
    primal_values = jnp.sum(exact_dot(flat, hot_low) * hot_high, axis=0, keepdims=True)
    coarse_send[...] = exact_dot(jnp.broadcast_to(primal_values, (8, count)), hot_coarse, NT)
    copies_d = send_pencil(lambda peer: coarse_send, coarse_in, d_send, d_recv)
    coarse_in[pencil] = coarse_send[...]
    finish(copies_d)
    coarse_send2[...] = sum(coarse_in[s] for s in range(pencils))
    copies_d2 = send_group(lambda peer: coarse_send2, coarse_in2, d2_send, d2_recv)
    coarse_in2[group] = coarse_send2[...]
    finish(copies_d2)
    coarse = sum(coarse_in2[h] for h in range(groups))
    lifted = exact_dot(coarse, inverse_ref[...], NT)
    added = exact_dot(lifted, hot_coarse)[0:1]
    added_rows = exact_dot(hot_high * added, hot_low, NT)
    for h in range(groups):
        picked[h] = picked[h] + added_rows[h * share_rows : (h + 1) * share_rows, :]
    copies_e = send_group(lambda peer: picked.at[peer], owner_in, e_send, e_recv)
    owner_in[group] = picked[group]
    finish(copies_e)

    owners = jnp.concatenate([owner_in[h] for h in range(groups)], axis=0)
    top, rest_part = halves(owners)
    owner_table = jnp.concatenate([top, rest_part], axis=1).astype(BF16)

    def image_step(block, carry):
        base = pl.multiple_of(block * 8, 8)
        lane_base = pl.multiple_of(block * 8 * LANES, 8 * LANES)
        pairs = pair_ref[:, pl.ds(lane_base, 8 * LANES)]
        high = lax.shift_right_logical(pairs, 7)
        low = jnp.bitwise_and(pairs, LANES - 1)
        found = []
        for i in range(8):
            lanes = slice(i * LANES, (i + 1) * LANES)
            hot = jnp.concatenate(
                [one_hot(low[0:1, lanes], LANES), one_hot(low[1:2, lanes], LANES)], axis=1
            )
            both = fast_dot(owner_table, jnp.concatenate([hot, hot], axis=0))
            place = iota((row_blocks, LANES), 0)
            jump = jnp.where(place == high[0:1, lanes], both[:, 0:LANES], 0.0) - jnp.where(
                place == high[1:2, lanes], both[:, LANES : 2 * LANES], 0.0
            )
            found.append(jnp.sum(jump, axis=0, keepdims=True))
        image[pl.ds(base, 8), :] = jnp.concatenate(found, axis=0)
        return carry

    lax.fori_loop(0, mult_rows // 8, image_step, 0)

    resid, search, scale, jumps = resid_ref[...], dir_ref[...], scale_ref[...], image[...]
    scaled_resid, scaled_jump = scale * resid, scale * jumps

    def lane_sums(values):
        return jnp.sum(values, axis=0, keepdims=True)

    sums_send[...] = jnp.concatenate(
        [
            lane_sums(resid * scaled_resid),
            lane_sums(search * jumps),
            lane_sums(scaled_resid * jumps),
            lane_sums(scaled_jump * jumps),
            jnp.zeros((4, LANES), F32),
        ],
        axis=0,
    )
    copies_f = send_pencil(lambda peer: sums_send, sums_in, f_send, f_recv)
    sums_in[pencil] = sums_send[...]
    finish(copies_f)
    sums_send2[...] = sum(sums_in[s] for s in range(pencils))
    copies_f2 = send_group(lambda peer: sums_send2, sums_in2, f2_send, f2_recv)
    sums_in2[group] = sums_send2[...]
    finish(copies_f2)
    totals = jnp.sum(sum(sums_in2[h] for h in range(groups)), axis=1, keepdims=True)
    old, curvature = totals[0:1], totals[1:2]
    alpha = old / curvature
    new = old - 2.0 * alpha * totals[2:3] + alpha * (alpha * totals[3:4])
    next_resid = resid - alpha * jumps
    iterate_out[...] = iterate_ref[...] + alpha * search
    resid_out[...] = next_resid
    dir_out[...] = scale * next_resid + (new / old) * search


def body(
    groups,
    pencils,
    mult_iterate,
    residual,
    direction,
    mult_scale,
    eigen_basis,
    eigen_values,
    elastic_coef,
    coarse_inverse,
    send_pos,
    pair_slots,
    prim_rows,
    coarse_idx,
):
    mult_count = direction.shape[-1]
    mult_rows = mult_count // LANES
    rows_count = send_pos.shape[-1]
    row_blocks = rows_count // LANES
    share_rows = row_blocks // groups
    patches, _, extent, _ = eigen_basis.shape
    comps = elastic_coef.shape[1]
    slab = extent // pencils
    slots = 4 * extent
    width = comps * extent // (pencils // patches)
    chunk = slab * comps
    table_rows = patches * chunk
    coarse_count = coarse_inverse.shape[0]

    def vmem(*shape):
        return pltpu.VMEM(shape, F32)

    def index(*shape):
        return pltpu.VMEM(shape, jnp.int32)

    share = (groups, share_rows, LANES)
    pencil_sems = pltpu.SemaphoreType.DMA((pencils,))
    group_sems = pltpu.SemaphoreType.DMA((groups,))
    scratch = [
        vmem(2 * row_blocks, LANES),
        vmem(*share),
        vmem(*share),
        index(*share),
        index(*share),
        vmem(2 * table_rows, slots),
        vmem(patches, chunk, slots),
        vmem(pencils, chunk, slots),
        vmem(slots, slots),
        vmem(slots, slots),
        vmem(comps * extent, width),
        vmem(slots, width),
        vmem(extent, width),
        vmem(extent, width),
        vmem(extent, width),
        vmem(slots, width),
        vmem(pencils, chunk, slots),
        vmem(pencils, chunk, slots),
        vmem(2 * table_rows, slots),
        vmem(*share),
        vmem(8, coarse_count),
        vmem(pencils, 8, coarse_count),
        vmem(8, coarse_count),
        vmem(groups, 8, coarse_count),
        vmem(*share),
        vmem(mult_rows, LANES),
        vmem(8, LANES),
        vmem(pencils, 8, LANES),
        vmem(8, LANES),
        vmem(groups, 8, LANES),
        group_sems,
        group_sems,
        pencil_sems,
        pencil_sems,
        pencil_sems,
        pencil_sems,
        pencil_sems,
        pencil_sems,
        group_sems,
        group_sems,
        group_sems,
        group_sems,
        pencil_sems,
        pencil_sems,
        group_sems,
        group_sems,
    ]
    shape = (mult_rows, LANES)
    outs = pl.pallas_call(
        functools.partial(kernel, groups, pencils),
        out_shape=[jax.ShapeDtypeStruct(shape, F32)] * 3,
        in_specs=[pl.BlockSpec(memory_space=pltpu.VMEM)] * 12,
        out_specs=[pl.BlockSpec(memory_space=pltpu.VMEM)] * 3,
        scratch_shapes=scratch,
        compiler_params=pltpu.CompilerParams(
            collective_id=0, has_side_effects=True, vmem_limit_bytes=48 * 1024 * 1024
        ),
        name="tearing_step",
    )(
        mult_iterate.reshape(shape),
        residual.reshape(shape),
        direction.reshape(shape),
        mult_scale.reshape(shape),
        eigen_basis,
        eigen_values,
        elastic_coef,
        coarse_inverse,
        send_pos.reshape(share),
        pair_slots.reshape(pair_slots.shape[2:]),
        prim_rows.reshape(1, -1),
        coarse_idx.reshape(1, -1),
    )
    return tuple(out.reshape(1, 1, mult_count) for out in outs)


def solution(mesh):
    rows = P("group", "pencil", None)
    in_specs = (
        rows,
        rows,
        rows,
        rows,
        P("group", None, None, None),
        P("group", None, None),
        P("group", None, None),
        P(),
        rows,
        P("group", "pencil", None, None),
        rows,
        rows,
    )
    return jax.shard_map(
        functools.partial(body, mesh.shape["group"], mesh.shape["pencil"]),
        mesh=mesh,
        in_specs=in_specs,
        out_specs=(rows, rows, rows),
        check_vma=False,
    )
```

time: 839 us -> 66.1 us (0.08)
  local copies, waits for them, and re-layouts: 521 us -> 9.04 us
  blocking collectives: 117 us -> 0 us
  waiting for transfers between devices: 85.3 us -> 0 us
  matrix products: 67.3 us -> 0 us
  Pallas kernels: 0 us -> 55.8 us
  starting transfers between devices: 20.1 us -> 0 us
  other arithmetic: 18.5 us -> 0 us
    gather x4 -> x0, local copies, waits for them, and re-layouts: 253 us -> none  [the longest x1 160 us: apply_inverse(): return volume_to_cycle(displace).reshape(-1)[positions]]
    scatter x3 -> x0, local copies, waits for them, and re-layouts: 124 us -> none  [the longest x2 63.1 us: body(): back_rows = jnp.zeros((rows_count,), jnp.float32).at[pair_rows[0]].set(se...]
    psum x3 -> x0, blocking collectives: 117 us -> none  [the longest x1 40.9 us: body(): norm_next = lax.psum(jnp.sum(resid_next * precond), ('group', 'pencil'))]
    all_to_all x4 -> x0, waiting for transfers between devices: 85.3 us -> none  [the longest x1 36.8 us: apply_inverse(): lax.all_to_all(mixed, 'pencil', split_axis=0, concat_axis=3, tiled=True)]
    dot_general x9 -> x0, matrix products: 67.3 us -> none  [the longest x1 14.1 us: apply_inverse(): jnp.einsum('xpcjk,pxi->ipcjk', columns, basis[:, 0], precision=highest)]
    pallas_call x0 -> x1, Pallas kernels: none -> 55.8 us  [body(): pl.pallas_call(functools.partial(kernel, groups, pencils), out_shape=[jax...]
    unnamed x26 -> x27, local copies, waits for them, and re-layouts: 63 us -> 9.04 us
    reshape x5 -> x0, local copies, waits for them, and re-layouts: 41.7 us -> none  [the longest x1 25.9 us: apply_inverse(): partial_yz.reshape(slab_x, patches, components, extent * extent)]
  transfers between devices with their start and end apart: 4 -> 0, of which waited for: 4 -> 0; matrix products, arithmetic and copies ran while one was open for 0% -> 0% of each run, Pallas kernels for 0% -> 0%
where the time goes in v1:
time: 66.1 us; the launch traced here: 65.5 us
  Pallas kernels  55.8 us (84%)
  local copies, waits for them, and re-layouts  9.04 us (14%)
  between operations  0.68 us (1%)
    pallas_call x1, Pallas kernels, body(): pl.pallas_call(functools.partial(kernel, groups, pencils), out_shape=[jax...  55.8 us
    unnamed x27, local copies, waits for them, and re-layouts  9.04 us

profile of v1, /device:TPU:0, one launch (start us, length us, event | category | flops | bytes accessed | tf_op | source)
XLA Modules:
  0.0 65.5 jit_solution(1637792580181795373)
XLA Ops:
  0.6 0.0 copy-start.10
  0.6 0.0 copy-start.4
  0.6 0.7 %copy-done.10 = f32[4,3,64]{2,0,1:T(4,128)S(1)} copy-done((f32[4,3,64]{2,0,1:T(4,128)S(1)}, f32[4,3,64]{2,0,1:T(4,128)}, u32[]{:S(2)}) %copy-start.10) | copy-done | bytes 3096
  1.3 0.0 copy-start.8
  1.3 0.0 copy-start.9
  1.3 0.7 %copy.16.coef_ref = f32[4,3,3]{2,1,0:T(4,128)S(1)} copy(f32[4,3,3]{2,0,1:T(4,128)} %param.18) | data formatting | bytes 288 | tf_op args[6]
  2.1 0.0 copy-done.4
  2.1 0.0 copy-done.8
  2.1 0.0 copy-done.9
  2.1 0.0 copy-start
  2.1 1.0 %copy-done = f32[4,3,64,64]{3,2,1,0:T(8,128)S(1)} copy-done((f32[4,3,64,64]{3,2,1,0:T(8,128)S(1)}, f32[4,3,64,64]{3,2,1,0:T(8,128)}, u32[]{:S(2)}) %copy-start) | copy-done | bytes 196632
  3.1 0.0 copy-start.1
  3.1 0.8 %copy-done.1 = f32[128,128]{1,0:T(8,128)S(1)} copy-done((f32[128,128]{1,0:T(8,128)S(1)}, f32[128,128]{1,0:T(8,128)}, u32[]{:S(2)}) %copy-start.1) | copy-done | bytes 65560
  3.9 0.0 copy-start.2
  3.9 0.8 %copy-done.2 = s32[1,1,16384]{2,1,0:T(1,128)S(1)} copy-done((s32[1,1,16384]{2,1,0:T(1,128)S(1)}, s32[1,1,16384]{2,1,0:T(1,128)}, u32[]{:S(2)}) %copy-start.2) | copy-done | bytes 65560
  4.7 0.0 copy-start.3
  4.7 0.8 %copy-done.3 = s32[1,1,2,8192]{3,2,1,0:T(2,128)S(1)} copy-done((s32[1,1,2,8192]{3,2,1,0:T(2,128)S(1)}, s32[1,1,2,8192]{3,2,1,0:T(2,128)}, u32[]{:S(2)}) %copy-start.3) | copy-done | bytes 65560
  5.6 0.0 copy-start.5
  5.6 0.8 %copy-done.5 = f32[1,1,8192]{2,1,0:T(1,128)S(1)} copy-done((f32[1,1,8192]{2,1,0:T(1,128)S(1)}, f32[1,1,8192]{2,1,0:T(1,128)}, u32[]{:S(2)}) %copy-start.5) | copy-done | bytes 32792
  6.3 0.0 copy-start.6
  6.3 0.8 %copy-done.6 = f32[1,1,8192]{2,1,0:T(1,128)S(1)} copy-done((f32[1,1,8192]{2,1,0:T(1,128)S(1)}, f32[1,1,8192]{2,1,0:T(1,128)}, u32[]{:S(2)}) %copy-start.6) | copy-done | bytes 32792
  7.1 0.0 copy-start.7
  7.1 0.8 %copy-done.7 = f32[1,1,8192]{2,1,0:T(1,128)S(1)} copy-done((f32[1,1,8192]{2,1,0:T(1,128)S(1)}, f32[1,1,8192]{2,1,0:T(1,128)}, u32[]{:S(2)}) %copy-start.7) | copy-done | bytes 32792
  7.9 55.8 %tearing_step.1 = (f32[64,128]{1,0:T(8,128)S(1)}, f32[64,128]{1,0:T(8,128)S(1)}, f32[64,128]{1,0:T(8,128)S(1)}) custom-call(f32[64,128]{1,0:T(8,128)S(1)} %bitcast.13, f32[64,128]{1,0:T(8,128)S(1)} %bitcast.14, f32[64,128]{1,0:T(8,128)S(1)} %bitcast.15, f32[64,128]{1,0:T(8,128)S(1)} %bitcast.16, f32[4,3,64,64]{3,2,1,0:T(8,128)S(1)} %copy-done, ...), custom_call_target="tpu_custom_call" | custom-call | tf_op jit(solution)/shard_map/tearing_step/pallas_call | solution.py:578
  63.7 0.6 copy.20
  64.3 0.6 copy.21
  64.9 0.6 copy.22
  (1 shorter events, 0.0 us)
Async XLA Ops:
  0.6 0.7 %copy-start.10 = (f32[4,3,64]{2,0,1:T(4,128)S(1)}, f32[4,3,64]{2,0,1:T(4,128)}, u32[]{:S(2)}) copy-start(f32[4,3,64]{2,0,1:T(4,128)} %param.17) | copy-start | bytes 9220
  0.6 1.4 %copy-start.4 = (f32[1,1,8192]{2,1,0:T(1,128)S(1)}, f32[1,1,8192]{2,1,0:T(1,128)}, u32[]{:S(2)}) copy-start(f32[1,1,8192]{2,1,0:T(1,128)} %param.12) | copy-start | bytes 98308
  1.3 0.7 %copy-start.8 = (s32[1,1,32]{2,1,0:T(1,128)S(1)}, s32[1,1,32]{2,1,0:T(1,128)}, u32[]{:S(2)}) copy-start(s32[1,1,32]{2,1,0:T(1,128)} %param.22) | copy-start | bytes 388
  1.3 0.7 %copy-start.9 = (s32[1,1,32]{2,1,0:T(1,128)S(1)}, s32[1,1,32]{2,1,0:T(1,128)}, u32[]{:S(2)}) copy-start(s32[1,1,32]{2,1,0:T(1,128)} %param.23) | copy-start | bytes 388
  2.1 1.0 %copy-start = (f32[4,3,64,64]{3,2,1,0:T(8,128)S(1)}, f32[4,3,64,64]{3,2,1,0:T(8,128)}, u32[]{:S(2)}) copy-start(f32[4,3,64,64]{3,2,1,0:T(8,128)} %basis_ref.1) | copy-start | bytes 589828
  3.1 0.8 %copy-start.1 = (f32[128,128]{1,0:T(8,128)S(1)}, f32[128,128]{1,0:T(8,128)}, u32[]{:S(2)}) copy-start(f32[128,128]{1,0:T(8,128)} %inverse_ref.1) | copy-start | bytes 196612
  3.9 0.8 %copy-start.2 = (s32[1,1,16384]{2,1,0:T(1,128)S(1)}, s32[1,1,16384]{2,1,0:T(1,128)}, u32[]{:S(2)}) copy-start(s32[1,1,16384]{2,1,0:T(1,128)} %param.20) | copy-start | bytes 196612
  4.7 0.8 %copy-start.3 = (s32[1,1,2,8192]{3,2,1,0:T(2,128)S(1)}, s32[1,1,2,8192]{3,2,1,0:T(2,128)}, u32[]{:S(2)}) copy-start(s32[1,1,2,8192]{3,2,1,0:T(2,128)} %param.21) | copy-start | bytes 196612
  5.6 0.8 %copy-start.5 = (f32[1,1,8192]{2,1,0:T(1,128)S(1)}, f32[1,1,8192]{2,1,0:T(1,128)}, u32[]{:S(2)}) copy-start(f32[1,1,8192]{2,1,0:T(1,128)} %param.13) | copy-start | bytes 98308
  6.3 0.8 %copy-start.6 = (f32[1,1,8192]{2,1,0:T(1,128)S(1)}, f32[1,1,8192]{2,1,0:T(1,128)}, u32[]{:S(2)}) copy-start(f32[1,1,8192]{2,1,0:T(1,128)} %param.14) | copy-start | bytes 98308
  7.1 0.8 %copy-start.7 = (f32[1,1,8192]{2,1,0:T(1,128)S(1)}, f32[1,1,8192]{2,1,0:T(1,128)}, u32[]{:S(2)}) copy-start(f32[1,1,8192]{2,1,0:T(1,128)} %param.15) | copy-start | bytes 98308

commit v2 on v1

--- a/solution.py
+++ b/solution.py
@@ -43,8 +43,24 @@
     return jnp.sum(jnp.where(diagonal, row, 0.0), axis=1, keepdims=True)
 
 
-def one_hot(rows, count):
-    return jnp.where(iota((count, rows.shape[1]), 0) == rows, 1.0, 0.0).astype(BF16)
+def numbers(count):
+    return iota((count, LANES), 0).astype(F32).astype(BF16).reshape(count // 16, 16, LANES)
+
+
+def packed(row):
+    return jnp.broadcast_to(row, (16, LANES)).astype(BF16)[None]
+
+
+def placed(counts, row, *values):
+    here = counts == packed(row)
+    size = counts.shape[0] * 16
+    zero = jnp.zeros((), BF16)
+    return [jnp.where(here, packed(value), zero).reshape(size, LANES) for value in values]
+
+
+def one_hot(counts, row):
+    here = counts == packed(row)
+    return jnp.where(here, jnp.ones((), BF16), jnp.zeros((), BF16)).reshape(-1, LANES)
 
 
 def block_diagonal(blocks):
@@ -65,21 +81,20 @@
 def kernel(
     groups,
     pencils,
-    iterate_ref,
-    resid_ref,
-    dir_ref,
-    scale_ref,
-    basis_ref,
-    values_ref,
-    coef_ref,
-    inverse_ref,
-    pos_ref,
-    pair_ref,
-    prim_ref,
-    cidx_ref,
-    iterate_out,
-    resid_out,
-    dir_out,
+    resid_hbm,
+    dir_hbm,
+    scale_hbm,
+    basis_hbm,
+    values_hbm,
+    coef_hbm,
+    inverse_hbm,
+    pos_hbm,
+    pair_hbm,
+    prim_hbm,
+    cidx_hbm,
+    image_out,
+    alpha_out,
+    beta_out,
     back_acc,
     back_send,
     rows_in,
@@ -126,11 +141,26 @@
     f_recv,
     f2_send,
     f2_recv,
+    resid_ref,
+    dir_ref,
+    scale_ref,
+    basis_ref,
+    values_ref,
+    coef_ref,
+    inverse_ref,
+    pos_ref,
+    pair_ref,
+    prim_ref,
+    cidx_ref,
+    xz_weight,
+    z_first,
+    z_last,
+    input_sem,
 ):
     group = lax.axis_index("group")
     pencil = lax.axis_index("pencil")
-    patches, _, extent, _ = basis_ref.shape
-    comps = coef_ref.shape[1]
+    patches, _, extent, _ = basis_hbm.shape
+    comps = coef_hbm.shape[0]
     slab = extent // pencils
     share_rows = pos_ref.shape[1]
     row_blocks = groups * share_rows
@@ -198,31 +228,57 @@
             barrier, inc=1, device_id=(group, pencil_peer(offset)), device_id_type=MESH
         )
 
+    inputs = {}
+    for number, (name, source, target) in enumerate(
+        [
+            ("dir", dir_hbm, dir_ref),
+            ("pair", pair_hbm, pair_ref),
+            ("pos", pos_hbm, pos_ref),
+            ("basis", basis_hbm.at[patch], basis_ref),
+            ("values", values_hbm, values_ref),
+            ("coef", coef_hbm, coef_ref),
+            ("prim", prim_hbm, prim_ref),
+            ("cidx", cidx_hbm, cidx_ref),
+            ("inverse", inverse_hbm, inverse_ref),
+            ("resid", resid_hbm, resid_ref),
+            ("scale", scale_hbm, scale_ref),
+        ]
+    ):
+        inputs[name] = pltpu.make_async_copy(source, target, input_sem.at[number])
+        inputs[name].start()
+
     back_acc[...] = jnp.zeros_like(back_acc)
+    row_numbers = numbers(row_blocks)
+    lane_numbers = numbers(LANES)
+    slot_numbers = numbers(slots)
+    table_numbers = numbers(table_rows)
+    inputs["dir"].wait()
+    inputs["pair"].wait()
 
     def back_step(block, carry):
         base = pl.multiple_of(block * 8, 8)
         lane_base = pl.multiple_of(block * 8 * LANES, 8 * LANES)
         values = dir_ref[pl.ds(base, 8), :]
         pairs = pair_ref[:, pl.ds(lane_base, 8 * LANES)]
-        high = lax.shift_right_logical(pairs, 7)
-        low = jnp.bitwise_and(pairs, LANES - 1)
+        high = lax.shift_right_logical(pairs, 7).astype(F32)
+        low = jnp.bitwise_and(pairs, LANES - 1).astype(F32)
         tops, rests = halves(values)
         left, right = [], []
         for i in range(8):
             lanes = slice(i * LANES, (i + 1) * LANES)
             for side, sign in ((0, 1.0), (1, -1.0)):
-                here = iota((row_blocks, LANES), 0) == high[side : side + 1, lanes]
                 left.append(
                     jnp.concatenate(
-                        [
-                            jnp.where(here, sign * tops[i : i + 1], 0.0).astype(BF16),
-                            jnp.where(here, sign * rests[i : i + 1], 0.0).astype(BF16),
-                        ],
+                        placed(
+                            row_numbers,
+                            high[side : side + 1, lanes],
+                            sign * tops[i : i + 1],
+                            sign * rests[i : i + 1],
+                        ),
                         axis=0,
                     )
                 )
-                right.append(one_hot(low[side : side + 1, lanes], LANES))
+                right.append(one_hot(lane_numbers, low[side : side + 1, lanes]))
         back_acc[...] += fast_dot(
             jnp.concatenate(left, axis=1), jnp.concatenate(right, axis=1), NT
         )
@@ -238,6 +294,8 @@
     copies_a = send_group(lambda peer: back_send.at[peer], rows_in, a_send, a_recv)
     rows_in[group] = back_send[group]
 
+    for name in ("pos", "basis", "values", "coef"):
+        inputs[name].wait()
     cells = pos_ref[...]
     cycle = 4 * extent - 4
     plane = floor_div(cells, cycle)
@@ -247,18 +305,23 @@
         + jnp.where(spot >= extent, 1, 0)
         + jnp.where(spot >= 2 * extent - 2, 2, 0)
         + jnp.where(spot >= 3 * extent - 4, 1, 0)
-    )
+    ).astype(F32)
     x_index = floor_div(plane, patches * comps)
     rest = plane - x_index * (patches * comps)
     p_index = floor_div(rest, comps)
     c_index = rest - p_index * comps
-    row_of[...] = p_index * chunk + c_index * slab + x_index
-
-    basis_x = basis_ref[patch, 0]
-    basis_y = basis_ref[patch, 1]
-    basis_z = basis_ref[patch, 2]
-    spectrum = values_ref[patch]
-    along_x = spectrum[0:1]
+    row_of[...] = (p_index * chunk + c_index * slab + x_index).astype(F32)
+
+    basis_x = basis_ref[0]
+    basis_y = basis_ref[1]
+    basis_z = basis_ref[2]
+
+    def of_patch(ref, row):
+        return sum(jnp.where(patch == p, ref[row, p : p + 1, :], 0.0) for p in range(patches))
+
+    spectrum = [of_patch(values_ref, axis) for axis in range(3)]
+    coef = [of_patch(coef_ref, c) for c in range(comps)]
+    along_x = spectrum[0]
     if dup > 1:
         basis_x = sum(
             jnp.where(part == u, basis_x[:, u * local_i : (u + 1) * local_i], 0.0)
@@ -272,18 +335,18 @@
     basis_yt, basis_zt = basis_y.T, basis_z.T
     diag_t[...] = block_diagonal([basis_zt, basis_yt, basis_yt, basis_zt])
     diag_x[...] = block_diagonal([basis_x] * comps)
-    coef = coef_ref[patch]
     ones = jnp.ones((1, local_i), F32)
-    weight_x = jnp.concatenate([coef[c : c + 1, 0:1] * along_x for c in range(comps)], axis=1)
-    weight_y = jnp.concatenate([coef[c : c + 1, 1:2] * ones for c in range(comps)], axis=1)
-    weight_z = jnp.concatenate([coef[c : c + 1, 2:3] * ones for c in range(comps)], axis=1)
-    y_weight[...] = column(spectrum[1:2]) * weight_y
+    weight_x = jnp.concatenate([coef[c][:, 0:1] * along_x for c in range(comps)], axis=1)
+    weight_y = jnp.concatenate([coef[c][:, 1:2] * ones for c in range(comps)], axis=1)
+    weight_z = jnp.concatenate([coef[c][:, 2:3] * ones for c in range(comps)], axis=1)
+    y_weight[...] = column(spectrum[1]) * weight_y
     wide = jnp.ones((1, width), F32)
     y_first[...] = column(basis_y[0:1]) * wide
     y_last[...] = column(basis_y[extent - 1 : extent]) * wide
-    xz_weight = weight_x + column(spectrum[2:3]) * weight_z
-    z_first = column(basis_z[0:1]) * wide
-    z_last = column(basis_z[extent - 1 : extent]) * wide
+    xz_weight[...] = weight_x + column(spectrum[2]) * weight_z
+    z_first[...] = column(basis_z[0:1]) * wide
+    z_last[...] = column(basis_z[extent - 1 : extent]) * wide
+    bwd[...] = jnp.zeros_like(bwd)
     load_acc[...] = jnp.zeros_like(load_acc)
     finish(copies_a)
 
@@ -293,17 +356,15 @@
         tops, rests = halves(values)
         left, right = [], []
         for i in range(share_rows):
-            here = iota((table_rows, LANES), 0) == rows[i : i + 1]
             left.append(
                 jnp.concatenate(
-                    [
-                        jnp.where(here, tops[i : i + 1], 0.0).astype(BF16),
-                        jnp.where(here, rests[i : i + 1], 0.0).astype(BF16),
-                    ],
+                    placed(
+                        table_numbers, rows[i : i + 1], tops[i : i + 1], rests[i : i + 1]
+                    ),
                     axis=0,
                 )
             )
-            right.append(one_hot(columns[i : i + 1], slots))
+            right.append(one_hot(slot_numbers, columns[i : i + 1]))
         load_acc[...] += fast_dot(
             jnp.concatenate(left, axis=1), jnp.concatenate(right, axis=1), NT
         )
@@ -324,36 +385,41 @@
         axis=0,
     )
     fwd[...] = exact_dot(exact_dot(diag_t[...], sides, NT), diag_x[...])
-    side_a = fwd[0:extent, :]
-    side_d = fwd[3 * extent : 4 * extent, :]
 
     def solve_step(block, carry):
-        sum_first, sum_last = carry
         base = pl.multiple_of(block * 8, 8)
         first = y_first[pl.ds(base, 8), :]
         last = y_last[pl.ds(base, 8), :]
         weight = y_weight[pl.ds(base, 8), :]
         side_b = fwd[pl.ds(extent + base, 8), :]
         side_c = fwd[pl.ds(2 * extent + base, 8), :]
-        out_b, out_c = [], []
-        for i in range(8):
-            row = slice(i, i + 1)
-            spectral = (
-                first[row] * side_a + last[row] * side_d + side_b[row] * z_first + side_c[row] * z_last
+        out_b, out_c = [None] * 8, [None] * 8
+        for k in range(0, extent, 8):
+            here = slice(k, k + 8)
+            there = slice(3 * extent + k, 3 * extent + k + 8)
+            side_a, side_d = fwd[here, :], fwd[there, :]
+            weights, z_one, z_two = xz_weight[here, :], z_first[here, :], z_last[here, :]
+            sum_first, sum_last = bwd[here, :], bwd[there, :]
+            for i in range(8):
+                row = slice(i, i + 1)
+                spectral = (
+                    first[row] * side_a + last[row] * side_d + side_b[row] * z_one + side_c[row] * z_two
+                )
+                scaled = spectral / (weights + weight[row])
+                sum_first = sum_first + first[row] * scaled
+                sum_last = sum_last + last[row] * scaled
+                term_b, term_c = z_one * scaled, z_two * scaled
+                out_b[i] = term_b if k == 0 else out_b[i] + term_b
+                out_c[i] = term_c if k == 0 else out_c[i] + term_c
+            bwd[here, :] = sum_first
+            bwd[there, :] = sum_last
+        for start, parts in ((extent, out_b), (2 * extent, out_c)):
+            bwd[pl.ds(start + base, 8), :] = jnp.concatenate(
+                [jnp.sum(part, axis=0, keepdims=True) for part in parts], axis=0
             )
-            scaled = spectral / (xz_weight + weight[row])
-            sum_first = sum_first + first[row] * scaled
-            sum_last = sum_last + last[row] * scaled
-            out_b.append(jnp.sum(z_first * scaled, axis=0, keepdims=True))
-            out_c.append(jnp.sum(z_last * scaled, axis=0, keepdims=True))
-        bwd[pl.ds(extent + base, 8), :] = jnp.concatenate(out_b, axis=0)
-        bwd[pl.ds(2 * extent + base, 8), :] = jnp.concatenate(out_c, axis=0)
-        return sum_first, sum_last
-
-    zero = jnp.zeros((extent, width), F32)
-    sum_first, sum_last = lax.fori_loop(0, extent // 8, solve_step, (zero, zero))
-    bwd[0:extent, :] = sum_first
-    bwd[3 * extent : 4 * extent, :] = sum_last
+        return carry
+
+    lax.fori_loop(0, extent // 8, solve_step, 0)
     cells_out = exact_dot(diag_x[...], exact_dot(diag[...], bwd[...]), NT)
     for s in range(pencils):
         out_send[s] = jnp.concatenate(
@@ -372,21 +438,25 @@
         for u in range(1, dup):
             total = total + out_in[p * dup + u]
         top, rest_part = halves(total)
-        table[p * chunk : (p + 1) * chunk, :] = top
-        table[table_rows + p * chunk : table_rows + (p + 1) * chunk, :] = rest_part
+        table[p * chunk : (p + 1) * chunk, 0:slots] = top
+        table[p * chunk : (p + 1) * chunk, slots : 2 * slots] = rest_part
     lookup = table[...].astype(BF16)
+    places = iota((table_rows, LANES), 0).astype(F32)
 
     def pick_step(h, carry):
         rows, columns = row_of[h], slot_of[h]
         found = []
         for i in range(0, share_rows, 2):
             hot = jnp.concatenate(
-                [one_hot(columns[i : i + 1], slots), one_hot(columns[i + 1 : i + 2], slots)], axis=1
+                [
+                    one_hot(slot_numbers, columns[i : i + 1]),
+                    one_hot(slot_numbers, columns[i + 1 : i + 2]),
+                ],
+                axis=1,
             )
-            both = fast_dot(lookup, hot)
-            both = both[0:table_rows] + both[table_rows : 2 * table_rows]
+            both = fast_dot(lookup, jnp.concatenate([hot, hot], axis=0))
             for u in range(2):
-                here = iota((table_rows, LANES), 0) == rows[i + u : i + u + 1]
+                here = places == rows[i + u : i + u + 1]
                 found.append(
                     jnp.sum(
                         jnp.where(here, both[:, u * LANES : (u + 1) * LANES], 0.0),
@@ -399,6 +469,8 @@
 
     lax.fori_loop(0, groups, pick_step, 0)
 
+    for name in ("prim", "cidx", "inverse"):
+        inputs[name].wait()
     primal = prim_ref[...]
     count = primal.shape[1]
     prim_high = lax.shift_right_logical(primal, 7)
@@ -436,12 +508,13 @@
         lane_base = pl.multiple_of(block * 8 * LANES, 8 * LANES)
         pairs = pair_ref[:, pl.ds(lane_base, 8 * LANES)]
         high = lax.shift_right_logical(pairs, 7)
-        low = jnp.bitwise_and(pairs, LANES - 1)
+        low = jnp.bitwise_and(pairs, LANES - 1).astype(F32)
         found = []
         for i in range(8):
             lanes = slice(i * LANES, (i + 1) * LANES)
             hot = jnp.concatenate(
-                [one_hot(low[0:1, lanes], LANES), one_hot(low[1:2, lanes], LANES)], axis=1
+                [one_hot(lane_numbers, low[0:1, lanes]), one_hot(lane_numbers, low[1:2, lanes])],
+                axis=1,
             )
             both = fast_dot(owner_table, jnp.concatenate([hot, hot], axis=0))
             place = iota((row_blocks, LANES), 0)
@@ -454,6 +527,8 @@
 
     lax.fori_loop(0, mult_rows // 8, image_step, 0)
 
+    for name in ("resid", "scale"):
+        inputs[name].wait()
     resid, search, scale, jumps = resid_ref[...], dir_ref[...], scale_ref[...], image[...]
     scaled_resid, scaled_jump = scale * resid, scale * jumps
 
@@ -481,10 +556,9 @@
     old, curvature = totals[0:1], totals[1:2]
     alpha = old / curvature
     new = old - 2.0 * alpha * totals[2:3] + alpha * (alpha * totals[3:4])
-    next_resid = resid - alpha * jumps
-    iterate_out[...] = iterate_ref[...] + alpha * search
-    resid_out[...] = next_resid
-    dir_out[...] = scale * next_resid + (new / old) * search
+    image_out[...] = jumps
+    alpha_out[...] = jnp.broadcast_to(alpha, alpha_out.shape)
+    beta_out[...] = jnp.broadcast_to(new / old, beta_out.shape)
 
 
 def body(
@@ -503,13 +577,14 @@
     prim_rows,
     coarse_idx,
 ):
-    mult_count = direction.shape[-1]
-    mult_rows = mult_count // LANES
+    mult_rows = direction.shape[-1] // LANES
     rows_count = send_pos.shape[-1]
     row_blocks = rows_count // LANES
     share_rows = row_blocks // groups
     patches, _, extent, _ = eigen_basis.shape
     comps = elastic_coef.shape[1]
+    pairs = pair_slots.reshape(pair_slots.shape[2:])
+    primal, coarse_ids = prim_rows.reshape(1, -1), coarse_idx.reshape(1, -1)
     slab = extent // pencils
     slots = 4 * extent
     width = comps * extent // (pencils // patches)
@@ -523,6 +598,7 @@
     def index(*shape):
         return pltpu.VMEM(shape, jnp.int32)
 
+    shape = (mult_rows, LANES)
     share = (groups, share_rows, LANES)
     pencil_sems = pltpu.SemaphoreType.DMA((pencils,))
     group_sems = pltpu.SemaphoreType.DMA((groups,))
@@ -530,8 +606,8 @@
         vmem(2 * row_blocks, LANES),
         vmem(*share),
         vmem(*share),
-        index(*share),
-        index(*share),
+        vmem(*share),
+        vmem(*share),
         vmem(2 * table_rows, slots),
         vmem(patches, chunk, slots),
         vmem(pencils, chunk, slots),
@@ -545,7 +621,7 @@
         vmem(slots, width),
         vmem(pencils, chunk, slots),
         vmem(pencils, chunk, slots),
-        vmem(2 * table_rows, slots),
+        vmem(table_rows, 2 * slots),
         vmem(*share),
         vmem(8, coarse_count),
         vmem(pencils, 8, coarse_count),
@@ -573,33 +649,50 @@
         pencil_sems,
         group_sems,
         group_sems,
+        vmem(*shape),
+        vmem(*shape),
+        vmem(*shape),
+        vmem(*eigen_basis.shape[1:]),
+        vmem(3, patches, extent),
+        vmem(comps, patches, 3),
+        vmem(coarse_count, coarse_count),
+        index(*share),
+        index(*pairs.shape),
+        index(*primal.shape),
+        index(*coarse_ids.shape),
+        vmem(extent, width),
+        vmem(extent, width),
+        vmem(extent, width),
+        pltpu.SemaphoreType.DMA((11,)),
     ]
-    shape = (mult_rows, LANES)
-    outs = pl.pallas_call(
+    image, alpha, beta = pl.pallas_call(
         functools.partial(kernel, groups, pencils),
         out_shape=[jax.ShapeDtypeStruct(shape, F32)] * 3,
-        in_specs=[pl.BlockSpec(memory_space=pltpu.VMEM)] * 12,
+        in_specs=[pl.BlockSpec(memory_space=pltpu.HBM)] * 11,
         out_specs=[pl.BlockSpec(memory_space=pltpu.VMEM)] * 3,
         scratch_shapes=scratch,
         compiler_params=pltpu.CompilerParams(
-            collective_id=0, has_side_effects=True, vmem_limit_bytes=48 * 1024 * 1024
+            collective_id=0, has_side_effects=True, vmem_limit_bytes=64 * 1024 * 1024 - 65536
         ),
         name="tearing_step",
     )(
-        mult_iterate.reshape(shape),
         residual.reshape(shape),
         direction.reshape(shape),
         mult_scale.reshape(shape),
         eigen_basis,
-        eigen_values,
-        elastic_coef,
+        eigen_values.transpose(1, 0, 2),
+        elastic_coef.transpose(1, 0, 2),
         coarse_inverse,
         send_pos.reshape(share),
-        pair_slots.reshape(pair_slots.shape[2:]),
-        prim_rows.reshape(1, -1),
-        coarse_idx.reshape(1, -1),
+        pairs,
+        primal,
+        coarse_ids,
     )
-    return tuple(out.reshape(1, 1, mult_count) for out in outs)
+    full = mult_iterate.shape
+    image, alpha, beta = image.reshape(full), alpha.reshape(full), beta.reshape(full)
+    next_resid = residual - alpha * image
+    next_dir = mult_scale * next_resid + beta * direction
+    return mult_iterate + alpha * direction, next_resid, next_dir
 
 
 def solution(mesh):

time: 66.1 us -> 58.4 us (0.88)
  local copies, waits for them, and re-layouts: 9.04 us -> 0 us
  other arithmetic: 0 us -> 1.61 us
    unnamed x27 -> x0, local copies, waits for them, and re-layouts: 9.04 us -> none
    add x0 -> x1, other arithmetic: none -> 1.61 us  [body(): next_dir = mult_scale * next_resid + beta * direction]
where the time goes in v2:
time: 58.4 us; the launch traced here: 58.2 us
  Pallas kernels  55.9 us (96%)
  other arithmetic  1.61 us (3%)
  between operations  0.64 us (1%)
    pallas_call x1, Pallas kernels, body(): pl.pallas_call(functools.partial(kernel, groups, pencils), out_shape=[jax...  55.9 us
    add x1, other arithmetic, body(): next_dir = mult_scale * next_resid + beta * direction  1.61 us

profile of v2, /device:TPU:0, one launch (start us, length us, event | category | flops | bytes accessed | tf_op | source)
XLA Modules:
  0.0 58.2 jit_solution(773907086481434904)
XLA Ops:
  0.6 55.9 %tearing_step.1 = (f32[64,128]{1,0:T(8,128)}, f32[64,128]{1,0:T(8,128)}, f32[64,128]{1,0:T(8,128)}) custom-call(f32[64,128]{1,0:T(8,128)} %bitcast.12, f32[64,128]{1,0:T(8,128)} %bitcast.13, f32[64,128]{1,0:T(8,128)} %bitcast.14, f32[4,3,64,64]{3,2,1,0:T(8,128)} %basis_hbm.1, f32[3,4,64]{2,1,0:T(4,128)} %bitcast.20, f32[3,4,3]{2,1,0:T(4,128)} %bitcast.21, ...), custom_call_target="tpu_custom_call" | custom-call | tf_op jit(solution)/shard_map/tearing_step/pallas_call | solution.py:668
  56.5 1.6 %multiply_add_fusion = (f32[1,1,8192]{2,1,0:T(1,128)}, f32[1,1,8192]{2,1,0:T(1,128)}, f32[1,1,8192]{2,1,0:T(1,128)}) fusion(f32[1,1,8192]{2,1,0:T(1,128)} %bitcast.19, f32[1,1,8192]{2,1,0:T(1,128)} %param.14, f32[1,1,8192]{2,1,0:T(1,128)} %param.15, f32[1,1,8192]{2,1,0:T(1,128)} %param.13, f32[1,1,8192]{2,1,0:T(1,128)} %bitcast.18, f32[1,1,8192]{2,1,0:T(1,128)} %bitcast.17, ...), kind=kLoop, calls=%fused_computation | loop fusion | flops 57344 | bytes 327680 | tf_op jit(solution)/shard_map/add | solution.py:694

commit v3 on v2

--- a/solution.py
+++ b/solution.py
@@ -117,14 +117,16 @@
     picked,
     coarse_send,
     coarse_in,
-    coarse_send2,
-    coarse_in2,
     owner_in,
     image,
     sums_send,
     sums_in,
-    sums_send2,
-    sums_in2,
+    info_send,
+    info_in,
+    inverse_acc,
+    hot_meets,
+    meet_rows,
+    meet_lanes,
     a_send,
     a_recv,
     b_send,
@@ -133,14 +135,12 @@
     c_recv,
     d_send,
     d_recv,
-    d2_send,
-    d2_recv,
+    i_send,
+    i_recv,
     e_send,
     e_recv,
     f_send,
     f_recv,
-    f2_send,
-    f2_recv,
     resid_ref,
     dir_ref,
     scale_ref,
@@ -173,6 +173,7 @@
     table_rows = patches * chunk
     patch = pencil // dup
     part = lax.rem(pencil, dup)
+    device = group * pencils + pencil
 
     def group_peer(offset):
         return lax.rem(group + offset, groups)
@@ -212,6 +213,26 @@
             copies.append(copy)
         return copies
 
+    def send_all(src, landing, send, recv):
+        copies = []
+        for g in range(groups):
+            for p in range(pencils):
+                if g == 0 and p == 0:
+                    continue
+                peer = (group_peer(g), pencil_peer(p))
+                copy = pltpu.make_async_remote_copy(
+                    src_ref=src,
+                    dst_ref=landing.at[device],
+                    send_sem=send.at[g * pencils + p],
+                    recv_sem=recv.at[g * pencils + p],
+                    device_id=peer,
+                    device_id_type=MESH,
+                )
+                copy.start()
+                copies.append(copy)
+        landing[device] = src[...]
+        return copies
+
     def finish(copies):
         for copy in copies:
             copy.wait_recv()
@@ -219,14 +240,15 @@
             copy.wait_send()
 
     barrier = pltpu.get_barrier_semaphore()
-    for offset in range(1, groups):
-        pl.semaphore_signal(
-            barrier, inc=1, device_id=(group_peer(offset), pencil), device_id_type=MESH
-        )
-    for offset in range(1, pencils):
-        pl.semaphore_signal(
-            barrier, inc=1, device_id=(group, pencil_peer(offset)), device_id_type=MESH
-        )
+    for g in range(groups):
+        for p in range(pencils):
+            if g or p:
+                pl.semaphore_signal(
+                    barrier,
+                    inc=1,
+                    device_id=(group_peer(g), pencil_peer(p)),
+                    device_id_type=MESH,
+                )
 
     inputs = {}
     for number, (name, source, target) in enumerate(
@@ -290,9 +312,19 @@
         low_rows = slice(row_blocks + h * share_rows, row_blocks + (h + 1) * share_rows)
         back_send[h] = back_acc[rows, :] + back_acc[low_rows, :]
 
-    pl.semaphore_wait(barrier, groups + pencils - 2)
+    pl.semaphore_wait(barrier, groups * pencils - 1)
     copies_a = send_group(lambda peer: back_send.at[peer], rows_in, a_send, a_recv)
     rows_in[group] = back_send[group]
+
+    for name in ("prim", "cidx"):
+        inputs[name].wait()
+    primal, coarse_ids = prim_ref[...], cidx_ref[...]
+    count = primal.shape[1]
+    info_send[...] = jnp.concatenate(
+        [primal.astype(F32), coarse_ids.astype(F32), jnp.zeros((6, count), F32)], axis=0
+    )
+    copies_i = send_group(lambda peer: info_send, info_in, i_send, i_recv)
+    info_in[group] = info_send[...]
 
     for name in ("pos", "basis", "values", "coef"):
         inputs[name].wait()
@@ -348,6 +380,35 @@
     z_last[...] = column(basis_z[extent - 1 : extent]) * wide
     bwd[...] = jnp.zeros_like(bwd)
     load_acc[...] = jnp.zeros_like(load_acc)
+
+    inverse_acc[...] = jnp.zeros_like(inverse_acc)
+    lane_of = iota((1, LANES), 1).astype(F32)
+
+    def inverse_step(block, carry):
+        lane_base = pl.multiple_of(block * 8 * LANES, 8 * LANES)
+        pairs = pair_ref[:, pl.ds(lane_base, 8 * LANES)]
+        high = lax.shift_right_logical(pairs, 7).astype(F32)
+        low = jnp.bitwise_and(pairs, LANES - 1).astype(F32)
+        first = jnp.zeros((1, LANES), F32) + (block * 8 + 1).astype(F32)
+        left, right = [], []
+        for i in range(8):
+            lanes = slice(i * LANES, (i + 1) * LANES)
+            for side, sign in ((0, 1.0), (1, -1.0)):
+                left.append(
+                    jnp.concatenate(
+                        placed(
+                            row_numbers, high[side : side + 1, lanes], sign * (first + i), lane_of
+                        ),
+                        axis=0,
+                    )
+                )
+                right.append(one_hot(lane_numbers, low[side : side + 1, lanes]))
+        inverse_acc[...] += fast_dot(
+            jnp.concatenate(left, axis=1), jnp.concatenate(right, axis=1), NT
+        )
+        return carry
+
+    lax.fori_loop(0, mult_rows // 8, inverse_step, 0)
     finish(copies_a)
 
     def load_step(h, carry):
@@ -378,6 +439,36 @@
         )
     copies_b = send_pencil(lambda peer: load_send.at[peer // dup], load_in, b_send, b_recv)
     load_in[pencil] = load_send[patch]
+
+    finish(copies_i)
+    all_rows = jnp.concatenate([info_in[h, 0:1, :] for h in range(groups)], axis=1)
+    all_ids = jnp.concatenate([info_in[h, 1:2, :] for h in range(groups)], axis=1)
+    owner = jnp.concatenate([jnp.full((1, count), h, F32) for h in range(groups)], axis=1)
+    share = share_rows * LANES
+    local = all_rows - (group * share).astype(F32)
+    mine = jnp.logical_and(local >= 0.0, local < share)
+    line = jnp.floor(local * (1.0 / LANES))
+    met_high = jnp.where(mine, owner * share_rows + line, -1.0)
+    met_low = local - line * LANES
+
+    def numbered(size):
+        return iota((size, groups * count), 0).astype(F32)
+
+    met_hot = jnp.where(numbered(LANES) == met_low, 1.0, 0.0).astype(BF16)
+    met_values = fast_dot(inverse_acc[...].astype(BF16), met_hot)
+    met_here = numbered(row_blocks) == met_high
+    met_row = jnp.sum(
+        jnp.where(met_here, met_values[0:row_blocks], 0.0), axis=0, keepdims=True
+    )
+    met_lane = jnp.sum(
+        jnp.where(met_here, met_values[row_blocks : 2 * row_blocks], 0.0), axis=0, keepdims=True
+    )
+    meet_rows[...] = jnp.where(
+        numbered(mult_rows) == jnp.abs(met_row) - 1.0, jnp.where(met_row > 0.0, 1.0, -1.0), 0.0
+    )
+    meet_lanes[...] = jnp.where(numbered(LANES) == met_lane, 1.0, 0.0)
+    coarse_count = inverse_hbm.shape[0]
+    hot_meets[...] = jnp.where(numbered(coarse_count) == all_ids, 1.0, 0.0)
     finish(copies_b)
 
     sides = jnp.concatenate(
@@ -469,34 +560,17 @@
 
     lax.fori_loop(0, groups, pick_step, 0)
 
-    for name in ("prim", "cidx", "inverse"):
-        inputs[name].wait()
-    primal = prim_ref[...]
-    count = primal.shape[1]
+    copies_e = send_group(lambda peer: picked.at[peer], owner_in, e_send, e_recv)
+    owner_in[group] = picked[group]
     prim_high = lax.shift_right_logical(primal, 7)
     prim_low = jnp.bitwise_and(primal, LANES - 1)
     hot_high = jnp.where(iota((row_blocks, count), 0) == prim_high, 1.0, 0.0)
     hot_low = jnp.where(iota((LANES, count), 0) == prim_low, 1.0, 0.0)
-    coarse_count = inverse_ref.shape[0]
-    hot_coarse = jnp.where(iota((coarse_count, count), 0) == cidx_ref[...], 1.0, 0.0)
+    hot_coarse = jnp.where(iota((coarse_count, count), 0) == coarse_ids, 1.0, 0.0)
     flat = jnp.concatenate([picked[h] for h in range(groups)], axis=0)
     primal_values = jnp.sum(exact_dot(flat, hot_low) * hot_high, axis=0, keepdims=True)
-    coarse_send[...] = exact_dot(jnp.broadcast_to(primal_values, (8, count)), hot_coarse, NT)
-    copies_d = send_pencil(lambda peer: coarse_send, coarse_in, d_send, d_recv)
-    coarse_in[pencil] = coarse_send[...]
-    finish(copies_d)
-    coarse_send2[...] = sum(coarse_in[s] for s in range(pencils))
-    copies_d2 = send_group(lambda peer: coarse_send2, coarse_in2, d2_send, d2_recv)
-    coarse_in2[group] = coarse_send2[...]
-    finish(copies_d2)
-    coarse = sum(coarse_in2[h] for h in range(groups))
-    lifted = exact_dot(coarse, inverse_ref[...], NT)
-    added = exact_dot(lifted, hot_coarse)[0:1]
-    added_rows = exact_dot(hot_high * added, hot_low, NT)
-    for h in range(groups):
-        picked[h] = picked[h] + added_rows[h * share_rows : (h + 1) * share_rows, :]
-    copies_e = send_group(lambda peer: picked.at[peer], owner_in, e_send, e_recv)
-    owner_in[group] = picked[group]
+    coarse_send[...] = exact_dot(jnp.broadcast_to(primal_values, (8, count)), hot_coarse, NT)[0:1]
+    copies_d = send_all(coarse_send, coarse_in, d_send, d_recv)
     finish(copies_e)
 
     owners = jnp.concatenate([owner_in[h] for h in range(groups)], axis=0)
@@ -527,35 +601,35 @@
 
     lax.fori_loop(0, mult_rows // 8, image_step, 0)
 
+    inputs["inverse"].wait()
+    finish(copies_d)
+    coarse = sum(coarse_in[d] for d in range(groups * pencils))
+    lifted = exact_dot(jnp.broadcast_to(coarse, (8, coarse_count)), inverse_ref[...], NT)
+    lifts = exact_dot(lifted, hot_meets[...])[0:1]
+    jump_lift = exact_dot(meet_rows[...] * lifts, meet_lanes[...], NT)
+
     for name in ("resid", "scale"):
         inputs[name].wait()
-    resid, search, scale, jumps = resid_ref[...], dir_ref[...], scale_ref[...], image[...]
+    resid, search, scale, jumps = resid_ref[...], dir_ref[...], scale_ref[...], image[...] + jump_lift
     scaled_resid, scaled_jump = scale * resid, scale * jumps
 
-    def lane_sums(values):
-        return jnp.sum(values, axis=0, keepdims=True)
-
-    sums_send[...] = jnp.concatenate(
-        [
-            lane_sums(resid * scaled_resid),
-            lane_sums(search * jumps),
-            lane_sums(scaled_resid * jumps),
-            lane_sums(scaled_jump * jumps),
-            jnp.zeros((4, LANES), F32),
-        ],
-        axis=0,
-    )
-    copies_f = send_pencil(lambda peer: sums_send, sums_in, f_send, f_recv)
-    sums_in[pencil] = sums_send[...]
-    finish(copies_f)
-    sums_send2[...] = sum(sums_in[s] for s in range(pencils))
-    copies_f2 = send_group(lambda peer: sums_send2, sums_in2, f2_send, f2_recv)
-    sums_in2[group] = sums_send2[...]
-    finish(copies_f2)
-    totals = jnp.sum(sum(sums_in2[h] for h in range(groups)), axis=1, keepdims=True)
-    old, curvature = totals[0:1], totals[1:2]
+    def total_of(values):
+        return jnp.sum(jnp.sum(values, axis=0, keepdims=True), axis=1, keepdims=True)
+
+    parts = [
+        total_of(resid * scaled_resid),
+        total_of(search * jumps),
+        total_of(scaled_resid * jumps),
+        total_of(scaled_jump * jumps),
+    ]
+    lane = iota((1, LANES), 1)
+    sums_send[...] = sum(jnp.where(lane == n, value, 0.0) for n, value in enumerate(parts))
+    finish(send_all(sums_send, sums_in, f_send, f_recv))
+    sums = sum(sums_in[d] for d in range(groups * pencils))
+    totals = [sums[:, n : n + 1] for n in range(4)]
+    old, curvature = totals[0], totals[1]
     alpha = old / curvature
-    new = old - 2.0 * alpha * totals[2:3] + alpha * (alpha * totals[3:4])
+    new = old - 2.0 * alpha * totals[2] + alpha * (alpha * totals[3])
     image_out[...] = jumps
     alpha_out[...] = jnp.broadcast_to(alpha, alpha_out.shape)
     beta_out[...] = jnp.broadcast_to(new / old, beta_out.shape)
@@ -591,6 +665,8 @@
     chunk = slab * comps
     table_rows = patches * chunk
     coarse_count = coarse_inverse.shape[0]
+    primal_count = primal.shape[1]
+    devices = groups * pencils
 
     def vmem(*shape):
         return pltpu.VMEM(shape, F32)
@@ -601,6 +677,7 @@
     shape = (mult_rows, LANES)
     share = (groups, share_rows, LANES)
     pencil_sems = pltpu.SemaphoreType.DMA((pencils,))
+    device_sems = pltpu.SemaphoreType.DMA((devices,))
     group_sems = pltpu.SemaphoreType.DMA((groups,))
     scratch = [
         vmem(2 * row_blocks, LANES),
@@ -623,32 +700,32 @@
         vmem(pencils, chunk, slots),
         vmem(table_rows, 2 * slots),
         vmem(*share),
-        vmem(8, coarse_count),
-        vmem(pencils, 8, coarse_count),
-        vmem(8, coarse_count),
-        vmem(groups, 8, coarse_count),
+        vmem(1, coarse_count),
+        vmem(devices, 1, coarse_count),
         vmem(*share),
         vmem(mult_rows, LANES),
-        vmem(8, LANES),
-        vmem(pencils, 8, LANES),
-        vmem(8, LANES),
-        vmem(groups, 8, LANES),
+        vmem(1, LANES),
+        vmem(devices, 1, LANES),
+        vmem(8, primal_count),
+        vmem(groups, 8, primal_count),
+        vmem(2 * row_blocks, LANES),
+        vmem(coarse_count, groups * primal_count),
+        vmem(mult_rows, groups * primal_count),
+        vmem(LANES, groups * primal_count),
         group_sems,
         group_sems,
         pencil_sems,
         pencil_sems,
         pencil_sems,
         pencil_sems,
-        pencil_sems,
-        pencil_sems,
+        device_sems,
+        device_sems,
         group_sems,
         group_sems,
         group_sems,
         group_sems,
-        pencil_sems,
-        pencil_sems,
-        group_sems,
-        group_sems,
+        device_sems,
+        device_sems,
         vmem(*shape),
         vmem(*shape),
         vmem(*shape),

time: 58.4 us -> 52.8 us (0.904)
  Pallas kernels: 55.9 us -> 50.3 us
    pallas_call x1, Pallas kernels: 55.9 us -> 50.3 us  [body(): pl.pallas_call(functools.partial(kernel, groups, pencils), out_shape=[jax...]
where the time goes in v3:
time: 52.8 us; the launch traced here: 52.6 us
  Pallas kernels  50.3 us (95%)
  other arithmetic  1.61 us (3%)
  between operations  0.64 us (1%)
    pallas_call x1, Pallas kernels, body(): pl.pallas_call(functools.partial(kernel, groups, pencils), out_shape=[jax...  50.3 us
    add x1, other arithmetic, body(): next_dir = mult_scale * next_resid + beta * direction  1.61 us

profile of v3, /device:TPU:0, one launch (start us, length us, event | category | flops | bytes accessed | tf_op | source)
XLA Modules:
  0.0 52.6 jit_solution(13076635851594892624)
XLA Ops:
  0.6 50.3 %tearing_step.1 = (f32[64,128]{1,0:T(8,128)}, f32[64,128]{1,0:T(8,128)}, f32[64,128]{1,0:T(8,128)}) custom-call(f32[64,128]{1,0:T(8,128)} %bitcast.12, f32[64,128]{1,0:T(8,128)} %bitcast.13, f32[64,128]{1,0:T(8,128)} %bitcast.14, f32[4,3,64,64]{3,2,1,0:T(8,128)} %basis_hbm.1, f32[3,4,64]{2,1,0:T(4,128)} %bitcast.20, f32[3,4,3]{2,1,0:T(4,128)} %bitcast.21, ...), custom_call_target="tpu_custom_call" | custom-call | tf_op jit(solution)/shard_map/tearing_step/pallas_call | solution.py:745
  51.0 1.6 %multiply_add_fusion = (f32[1,1,8192]{2,1,0:T(1,128)}, f32[1,1,8192]{2,1,0:T(1,128)}, f32[1,1,8192]{2,1,0:T(1,128)}) fusion(f32[1,1,8192]{2,1,0:T(1,128)} %bitcast.19, f32[1,1,8192]{2,1,0:T(1,128)} %param.14, f32[1,1,8192]{2,1,0:T(1,128)} %param.15, f32[1,1,8192]{2,1,0:T(1,128)} %param.13, f32[1,1,8192]{2,1,0:T(1,128)} %bitcast.18, f32[1,1,8192]{2,1,0:T(1,128)} %bitcast.17, ...), kind=kLoop, calls=%fused_computation | loop fusion | flops 57344 | bytes 327680 | tf_op jit(solution)/shard_map/add | solution.py:771

commit v4 on v3

--- a/solution.py
+++ b/solution.py
@@ -10,16 +10,11 @@
 LANES = 128
 F32 = jnp.float32
 BF16 = jnp.bfloat16
-HIGHEST = lax.Precision.HIGHEST
 MESH = pl.DeviceIdType.MESH
 NT = (((1,), (1,)), ((), ()))
 NN = (((1,), (0,)), ((), ()))
 
 
-def exact_dot(left, right, dims=NN):
-    return lax.dot_general(left, right, dims, precision=HIGHEST, preferred_element_type=F32)
-
-
 def fast_dot(left, right, dims=NN):
     return lax.dot_general(left, right, dims, preferred_element_type=F32)
 
@@ -27,6 +22,22 @@
 def halves(values):
     top = values.astype(BF16).astype(F32)
     return top, values - top
+
+
+def split_dot(left, right, dims=NN):
+    left_top, left_rest = (half.astype(BF16) for half in halves(left))
+    right_top, right_rest = (half.astype(BF16) for half in halves(right))
+    return (
+        fast_dot(left_top, right_top, dims)
+        + fast_dot(left_top, right_rest, dims)
+        + fast_dot(left_rest, right_top, dims)
+    )
+
+
+def hot_dot(left, right, dims=NN):
+    top, rest = (half.astype(BF16) for half in halves(left))
+    hot = right.astype(BF16)
+    return fast_dot(top, hot, dims) + fast_dot(rest, hot, dims)
 
 
 def floor_div(values, divisor):
@@ -181,18 +192,21 @@
     def pencil_peer(offset):
         return lax.rem(pencil + offset, pencils)
 
+    def group_copy(src, landing, send, recv, offset, peer):
+        return pltpu.make_async_remote_copy(
+            src_ref=src,
+            dst_ref=landing.at[group],
+            send_sem=send.at[offset],
+            recv_sem=recv.at[offset],
+            device_id=(peer, pencil),
+            device_id_type=MESH,
+        )
+
     def send_group(src_of, landing, send, recv):
         copies = []
         for offset in range(1, groups):
             peer = group_peer(offset)
-            copy = pltpu.make_async_remote_copy(
-                src_ref=src_of(peer),
-                dst_ref=landing.at[group],
-                send_sem=send.at[offset],
-                recv_sem=recv.at[offset],
-                device_id=(peer, pencil),
-                device_id_type=MESH,
-            )
+            copy = group_copy(src_of(peer), landing, send, recv, offset, peer)
             copy.start()
             copies.append(copy)
         return copies
@@ -326,8 +340,7 @@
     copies_i = send_group(lambda peer: info_send, info_in, i_send, i_recv)
     info_in[group] = info_send[...]
 
-    for name in ("pos", "basis", "values", "coef"):
-        inputs[name].wait()
+    inputs["pos"].wait()
     cells = pos_ref[...]
     cycle = 4 * extent - 4
     plane = floor_div(cells, cycle)
@@ -344,6 +357,48 @@
     c_index = rest - p_index * comps
     row_of[...] = (p_index * chunk + c_index * slab + x_index).astype(F32)
 
+    load_acc[...] = jnp.zeros_like(load_acc)
+
+
+    def load_step(offset, carry):
+        h = lax.rem(group - offset + groups, groups)
+        group_copy(back_send.at[h], rows_in, a_send, a_recv, offset, h).wait_recv()
+        load_from(h)
+        return carry
+
+    def load_from(h):
+        values = rows_in[h]
+        rows, columns = row_of[h], slot_of[h]
+        tops, rests = halves(values)
+        left, right = [], []
+        for i in range(share_rows):
+            left.append(
+                jnp.concatenate(
+                    placed(
+                        table_numbers, rows[i : i + 1], tops[i : i + 1], rests[i : i + 1]
+                    ),
+                    axis=0,
+                )
+            )
+            right.append(one_hot(slot_numbers, columns[i : i + 1]))
+        load_acc[...] += fast_dot(
+            jnp.concatenate(left, axis=1), jnp.concatenate(right, axis=1), NT
+        )
+
+    load_from(group)
+    lax.fori_loop(1, groups, load_step, 0)
+    for copy in copies_a:
+        copy.wait_send()
+    for p in range(patches):
+        load_send[p] = (
+            load_acc[p * chunk : (p + 1) * chunk, :]
+            + load_acc[table_rows + p * chunk : table_rows + (p + 1) * chunk, :]
+        )
+    copies_b = send_pencil(lambda peer: load_send.at[peer // dup], load_in, b_send, b_recv)
+    load_in[pencil] = load_send[patch]
+
+    for name in ("basis", "values", "coef"):
+        inputs[name].wait()
     basis_x = basis_ref[0]
     basis_y = basis_ref[1]
     basis_z = basis_ref[2]
@@ -379,8 +434,6 @@
     z_first[...] = column(basis_z[0:1]) * wide
     z_last[...] = column(basis_z[extent - 1 : extent]) * wide
     bwd[...] = jnp.zeros_like(bwd)
-    load_acc[...] = jnp.zeros_like(load_acc)
-
     inverse_acc[...] = jnp.zeros_like(inverse_acc)
     lane_of = iota((1, LANES), 1).astype(F32)
 
@@ -409,73 +462,13 @@
         return carry
 
     lax.fori_loop(0, mult_rows // 8, inverse_step, 0)
-    finish(copies_a)
-
-    def load_step(h, carry):
-        values = rows_in[h]
-        rows, columns = row_of[h], slot_of[h]
-        tops, rests = halves(values)
-        left, right = [], []
-        for i in range(share_rows):
-            left.append(
-                jnp.concatenate(
-                    placed(
-                        table_numbers, rows[i : i + 1], tops[i : i + 1], rests[i : i + 1]
-                    ),
-                    axis=0,
-                )
-            )
-            right.append(one_hot(slot_numbers, columns[i : i + 1]))
-        load_acc[...] += fast_dot(
-            jnp.concatenate(left, axis=1), jnp.concatenate(right, axis=1), NT
-        )
-        return carry
-
-    lax.fori_loop(0, groups, load_step, 0)
-    for p in range(patches):
-        load_send[p] = (
-            load_acc[p * chunk : (p + 1) * chunk, :]
-            + load_acc[table_rows + p * chunk : table_rows + (p + 1) * chunk, :]
-        )
-    copies_b = send_pencil(lambda peer: load_send.at[peer // dup], load_in, b_send, b_recv)
-    load_in[pencil] = load_send[patch]
-
-    finish(copies_i)
-    all_rows = jnp.concatenate([info_in[h, 0:1, :] for h in range(groups)], axis=1)
-    all_ids = jnp.concatenate([info_in[h, 1:2, :] for h in range(groups)], axis=1)
-    owner = jnp.concatenate([jnp.full((1, count), h, F32) for h in range(groups)], axis=1)
-    share = share_rows * LANES
-    local = all_rows - (group * share).astype(F32)
-    mine = jnp.logical_and(local >= 0.0, local < share)
-    line = jnp.floor(local * (1.0 / LANES))
-    met_high = jnp.where(mine, owner * share_rows + line, -1.0)
-    met_low = local - line * LANES
-
-    def numbered(size):
-        return iota((size, groups * count), 0).astype(F32)
-
-    met_hot = jnp.where(numbered(LANES) == met_low, 1.0, 0.0).astype(BF16)
-    met_values = fast_dot(inverse_acc[...].astype(BF16), met_hot)
-    met_here = numbered(row_blocks) == met_high
-    met_row = jnp.sum(
-        jnp.where(met_here, met_values[0:row_blocks], 0.0), axis=0, keepdims=True
-    )
-    met_lane = jnp.sum(
-        jnp.where(met_here, met_values[row_blocks : 2 * row_blocks], 0.0), axis=0, keepdims=True
-    )
-    meet_rows[...] = jnp.where(
-        numbered(mult_rows) == jnp.abs(met_row) - 1.0, jnp.where(met_row > 0.0, 1.0, -1.0), 0.0
-    )
-    meet_lanes[...] = jnp.where(numbered(LANES) == met_lane, 1.0, 0.0)
-    coarse_count = inverse_hbm.shape[0]
-    hot_meets[...] = jnp.where(numbered(coarse_count) == all_ids, 1.0, 0.0)
     finish(copies_b)
 
     sides = jnp.concatenate(
         [load_in[s, c * slab : (c + 1) * slab, :] for c in range(comps) for s in range(pencils)],
         axis=0,
     )
-    fwd[...] = exact_dot(exact_dot(diag_t[...], sides, NT), diag_x[...])
+    fwd[...] = split_dot(split_dot(diag_t[...], sides, NT), diag_x[...])
 
     def solve_step(block, carry):
         base = pl.multiple_of(block * 8, 8)
@@ -511,7 +504,7 @@
         return carry
 
     lax.fori_loop(0, extent // 8, solve_step, 0)
-    cells_out = exact_dot(diag_x[...], exact_dot(diag[...], bwd[...]), NT)
+    cells_out = split_dot(diag_x[...], split_dot(diag[...], bwd[...]), NT)
     for s in range(pencils):
         out_send[s] = jnp.concatenate(
             [
@@ -522,6 +515,35 @@
         )
     copies_c = send_pencil(lambda peer: out_send.at[peer], out_in, c_send, c_recv)
     out_in[pencil] = out_send[pencil]
+    finish(copies_i)
+    all_rows = jnp.concatenate([info_in[h, 0:1, :] for h in range(groups)], axis=1)
+    all_ids = jnp.concatenate([info_in[h, 1:2, :] for h in range(groups)], axis=1)
+    owner = jnp.concatenate([jnp.full((1, count), h, F32) for h in range(groups)], axis=1)
+    share = share_rows * LANES
+    local = all_rows - (group * share).astype(F32)
+    mine = jnp.logical_and(local >= 0.0, local < share)
+    line = jnp.floor(local * (1.0 / LANES))
+    met_high = jnp.where(mine, owner * share_rows + line, -1.0)
+    met_low = local - line * LANES
+
+    def numbered(size):
+        return iota((size, groups * count), 0).astype(F32)
+
+    met_hot = jnp.where(numbered(LANES) == met_low, 1.0, 0.0).astype(BF16)
+    met_values = fast_dot(inverse_acc[...].astype(BF16), met_hot)
+    met_here = numbered(row_blocks) == met_high
+    met_row = jnp.sum(
+        jnp.where(met_here, met_values[0:row_blocks], 0.0), axis=0, keepdims=True
+    )
+    met_lane = jnp.sum(
+        jnp.where(met_here, met_values[row_blocks : 2 * row_blocks], 0.0), axis=0, keepdims=True
+    )
+    meet_rows[...] = jnp.where(
+        numbered(mult_rows) == jnp.abs(met_row) - 1.0, jnp.where(met_row > 0.0, 1.0, -1.0), 0.0
+    )
+    meet_lanes[...] = jnp.where(numbered(LANES) == met_lane, 1.0, 0.0)
+    coarse_count = inverse_hbm.shape[0]
+    hot_meets[...] = jnp.where(numbered(coarse_count) == all_ids, 1.0, 0.0)
     finish(copies_c)
 
     for p in range(patches):
@@ -534,7 +556,13 @@
     lookup = table[...].astype(BF16)
     places = iota((table_rows, LANES), 0).astype(F32)
 
-    def pick_step(h, carry):
+    def pick_step(offset, carry):
+        peer = group_peer(offset)
+        pick_for(peer)
+        group_copy(picked.at[peer], owner_in, e_send, e_recv, offset, peer).start()
+        return carry
+
+    def pick_for(h):
         rows, columns = row_of[h], slot_of[h]
         found = []
         for i in range(0, share_rows, 2):
@@ -556,11 +584,10 @@
                     )
                 )
         picked[h] = jnp.concatenate(found, axis=0)
-        return carry
-
-    lax.fori_loop(0, groups, pick_step, 0)
-
-    copies_e = send_group(lambda peer: picked.at[peer], owner_in, e_send, e_recv)
+
+    lax.fori_loop(1, groups, pick_step, 0)
+    pick_for(group)
+
     owner_in[group] = picked[group]
     prim_high = lax.shift_right_logical(primal, 7)
     prim_low = jnp.bitwise_and(primal, LANES - 1)
@@ -568,10 +595,17 @@
     hot_low = jnp.where(iota((LANES, count), 0) == prim_low, 1.0, 0.0)
     hot_coarse = jnp.where(iota((coarse_count, count), 0) == coarse_ids, 1.0, 0.0)
     flat = jnp.concatenate([picked[h] for h in range(groups)], axis=0)
-    primal_values = jnp.sum(exact_dot(flat, hot_low) * hot_high, axis=0, keepdims=True)
-    coarse_send[...] = exact_dot(jnp.broadcast_to(primal_values, (8, count)), hot_coarse, NT)[0:1]
+    primal_values = jnp.sum(hot_dot(flat, hot_low) * hot_high, axis=0, keepdims=True)
+    coarse_send[...] = hot_dot(jnp.broadcast_to(primal_values, (8, count)), hot_coarse, NT)[0:1]
     copies_d = send_all(coarse_send, coarse_in, d_send, d_recv)
-    finish(copies_e)
+    finish(
+        [
+            group_copy(
+                picked.at[group_peer(offset)], owner_in, e_send, e_recv, offset, group_peer(offset)
+            )
+            for offset in range(1, groups)
+        ]
+    )
 
     owners = jnp.concatenate([owner_in[h] for h in range(groups)], axis=0)
     top, rest_part = halves(owners)
@@ -604,9 +638,9 @@
     inputs["inverse"].wait()
     finish(copies_d)
     coarse = sum(coarse_in[d] for d in range(groups * pencils))
-    lifted = exact_dot(jnp.broadcast_to(coarse, (8, coarse_count)), inverse_ref[...], NT)
-    lifts = exact_dot(lifted, hot_meets[...])[0:1]
-    jump_lift = exact_dot(meet_rows[...] * lifts, meet_lanes[...], NT)
+    lifted = split_dot(jnp.broadcast_to(coarse, (8, coarse_count)), inverse_ref[...], NT)
+    lifts = hot_dot(lifted, hot_meets[...])[0:1]
+    jump_lift = hot_dot(meet_rows[...] * lifts, meet_lanes[...], NT)
 
     for name in ("resid", "scale"):
         inputs[name].wait()

time: 52.8 us -> 49.8 us (0.943)
  Pallas kernels: 50.3 us -> 47.3 us
    pallas_call x1, Pallas kernels: 50.3 us -> 47.3 us  [body(): pl.pallas_call(functools.partial(kernel, groups, pencils), out_shape=[jax...]
where the time goes in v4:
time: 49.8 us; the launch traced here: 49.6 us
  Pallas kernels  47.3 us (95%)
  other arithmetic  1.61 us (3%)
  between operations  0.64 us (1%)
    pallas_call x1, Pallas kernels, body(): pl.pallas_call(functools.partial(kernel, groups, pencils), out_shape=[jax...  47.3 us
    add x1, other arithmetic, body(): next_dir = mult_scale * next_resid + beta * direction  1.61 us

profile of v4, /device:TPU:0, one launch (start us, length us, event | category | flops | bytes accessed | tf_op | source)
XLA Modules:
  0.0 49.6 jit_solution(8278112166818315932)
XLA Ops:
  0.6 47.3 %tearing_step.1 = (f32[64,128]{1,0:T(8,128)}, f32[64,128]{1,0:T(8,128)}, f32[64,128]{1,0:T(8,128)}) custom-call(f32[64,128]{1,0:T(8,128)} %bitcast.12, f32[64,128]{1,0:T(8,128)} %bitcast.13, f32[64,128]{1,0:T(8,128)} %bitcast.14, f32[4,3,64,64]{3,2,1,0:T(8,128)} %basis_hbm.1, f32[3,4,64]{2,1,0:T(4,128)} %bitcast.20, f32[3,4,3]{2,1,0:T(4,128)} %bitcast.21, ...), custom_call_target="tpu_custom_call" | custom-call | tf_op jit(solution)/shard_map/tearing_step/pallas_call | solution.py:779
  48.0 1.6 %multiply_add_fusion = (f32[1,1,8192]{2,1,0:T(1,128)}, f32[1,1,8192]{2,1,0:T(1,128)}, f32[1,1,8192]{2,1,0:T(1,128)}) fusion(f32[1,1,8192]{2,1,0:T(1,128)} %bitcast.19, f32[1,1,8192]{2,1,0:T(1,128)} %param.14, f32[1,1,8192]{2,1,0:T(1,128)} %param.15, f32[1,1,8192]{2,1,0:T(1,128)} %param.13, f32[1,1,8192]{2,1,0:T(1,128)} %bitcast.18, f32[1,1,8192]{2,1,0:T(1,128)} %bitcast.17, ...), kind=kLoop, calls=%fused_computation | loop fusion | flops 57344 | bytes 327680 | tf_op jit(solution)/shard_map/add | solution.py:805

commit v5 on v4

--- a/solution.py
+++ b/solution.py
@@ -227,25 +227,32 @@
             copies.append(copy)
         return copies
 
+    def device_peer(number):
+        return group_peer(number // pencils), pencil_peer(lax.rem(number, pencils))
+
+    def all_copy(src, landing, send, recv, number):
+        return pltpu.make_async_remote_copy(
+            src_ref=src,
+            dst_ref=landing.at[device],
+            send_sem=send.at[number],
+            recv_sem=recv.at[number],
+            device_id=device_peer(number),
+            device_id_type=MESH,
+        )
+
+    def each_device(action):
+        def step(number, carry):
+            action(number)
+            return carry
+
+        lax.fori_loop(1, groups * pencils, step, 0)
+
     def send_all(src, landing, send, recv):
-        copies = []
-        for g in range(groups):
-            for p in range(pencils):
-                if g == 0 and p == 0:
-                    continue
-                peer = (group_peer(g), pencil_peer(p))
-                copy = pltpu.make_async_remote_copy(
-                    src_ref=src,
-                    dst_ref=landing.at[device],
-                    send_sem=send.at[g * pencils + p],
-                    recv_sem=recv.at[g * pencils + p],
-                    device_id=peer,
-                    device_id_type=MESH,
-                )
-                copy.start()
-                copies.append(copy)
+        each_device(lambda number: all_copy(src, landing, send, recv, number).start())
         landing[device] = src[...]
-        return copies
+
+    def finish_all(src, landing, send, recv):
+        each_device(lambda number: all_copy(src, landing, send, recv, number).wait())
 
     def finish(copies):
         for copy in copies:
@@ -254,15 +261,11 @@
             copy.wait_send()
 
     barrier = pltpu.get_barrier_semaphore()
-    for g in range(groups):
-        for p in range(pencils):
-            if g or p:
-                pl.semaphore_signal(
-                    barrier,
-                    inc=1,
-                    device_id=(group_peer(g), pencil_peer(p)),
-                    device_id_type=MESH,
-                )
+    each_device(
+        lambda number: pl.semaphore_signal(
+            barrier, inc=1, device_id=device_peer(number), device_id_type=MESH
+        )
+    )
 
     inputs = {}
     for number, (name, source, target) in enumerate(
@@ -362,11 +365,11 @@
 
     def load_step(offset, carry):
         h = lax.rem(group - offset + groups, groups)
-        group_copy(back_send.at[h], rows_in, a_send, a_recv, offset, h).wait_recv()
-        load_from(h)
-        return carry
-
-    def load_from(h):
+
+        @pl.when(offset > 0)
+        def _():
+            group_copy(back_send.at[h], rows_in, a_send, a_recv, offset, h).wait_recv()
+
         values = rows_in[h]
         rows, columns = row_of[h], slot_of[h]
         tops, rests = halves(values)
@@ -384,9 +387,9 @@
         load_acc[...] += fast_dot(
             jnp.concatenate(left, axis=1), jnp.concatenate(right, axis=1), NT
         )
-
-    load_from(group)
-    lax.fori_loop(1, groups, load_step, 0)
+        return carry
+
+    lax.fori_loop(0, groups, load_step, 0)
     for copy in copies_a:
         copy.wait_send()
     for p in range(patches):
@@ -477,26 +480,34 @@
         weight = y_weight[pl.ds(base, 8), :]
         side_b = fwd[pl.ds(extent + base, 8), :]
         side_c = fwd[pl.ds(2 * extent + base, 8), :]
-        out_b, out_c = [None] * 8, [None] * 8
-        for k in range(0, extent, 8):
-            here = slice(k, k + 8)
-            there = slice(3 * extent + k, 3 * extent + k + 8)
-            side_a, side_d = fwd[here, :], fwd[there, :]
-            weights, z_one, z_two = xz_weight[here, :], z_first[here, :], z_last[here, :]
-            sum_first, sum_last = bwd[here, :], bwd[there, :]
-            for i in range(8):
-                row = slice(i, i + 1)
+        out_b, out_c = [], []
+        for i in range(8):
+            row = slice(i, i + 1)
+            row_first = jnp.broadcast_to(first[row], (8, width))
+            row_last = jnp.broadcast_to(last[row], (8, width))
+            row_weight = jnp.broadcast_to(weight[row], (8, width))
+            row_b = jnp.broadcast_to(side_b[row], (8, width))
+            row_c = jnp.broadcast_to(side_c[row], (8, width))
+            sum_b = sum_c = jnp.zeros((8, width), F32)
+            for k in range(0, extent, 8):
+                here = slice(k, k + 8)
+                there = slice(3 * extent + k, 3 * extent + k + 8)
+                z_one, z_two = z_first[here, :], z_last[here, :]
                 spectral = (
-                    first[row] * side_a + last[row] * side_d + side_b[row] * z_one + side_c[row] * z_two
+                    row_first * fwd[here, :]
+                    + row_last * fwd[there, :]
+                    + row_b * z_one
+                    + row_c * z_two
                 )
-                scaled = spectral / (weights + weight[row])
-                sum_first = sum_first + first[row] * scaled
-                sum_last = sum_last + last[row] * scaled
-                term_b, term_c = z_one * scaled, z_two * scaled
-                out_b[i] = term_b if k == 0 else out_b[i] + term_b
-                out_c[i] = term_c if k == 0 else out_c[i] + term_c
-            bwd[here, :] = sum_first
-            bwd[there, :] = sum_last
+                weights = xz_weight[here, :] + row_weight
+                guess = pl.reciprocal(weights, approx=True)
+                scaled = spectral * (guess * (2.0 - weights * guess))
+                bwd[here, :] += row_first * scaled
+                bwd[there, :] += row_last * scaled
+                sum_b = sum_b + z_one * scaled
+                sum_c = sum_c + z_two * scaled
+            out_b.append(sum_b)
+            out_c.append(sum_c)
         for start, parts in ((extent, out_b), (2 * extent, out_c)):
             bwd[pl.ds(start + base, 8), :] = jnp.concatenate(
                 [jnp.sum(part, axis=0, keepdims=True) for part in parts], axis=0
@@ -557,12 +568,7 @@
     places = iota((table_rows, LANES), 0).astype(F32)
 
     def pick_step(offset, carry):
-        peer = group_peer(offset)
-        pick_for(peer)
-        group_copy(picked.at[peer], owner_in, e_send, e_recv, offset, peer).start()
-        return carry
-
-    def pick_for(h):
+        h = group_peer(offset)
         rows, columns = row_of[h], slot_of[h]
         found = []
         for i in range(0, share_rows, 2):
@@ -585,8 +591,13 @@
                 )
         picked[h] = jnp.concatenate(found, axis=0)
 
-    lax.fori_loop(1, groups, pick_step, 0)
-    pick_for(group)
+        @pl.when(offset < groups)
+        def _():
+            group_copy(picked.at[h], owner_in, e_send, e_recv, offset, h).start()
+
+        return carry
+
+    lax.fori_loop(1, groups + 1, pick_step, 0)
 
     owner_in[group] = picked[group]
     prim_high = lax.shift_right_logical(primal, 7)
@@ -597,7 +608,7 @@
     flat = jnp.concatenate([picked[h] for h in range(groups)], axis=0)
     primal_values = jnp.sum(hot_dot(flat, hot_low) * hot_high, axis=0, keepdims=True)
     coarse_send[...] = hot_dot(jnp.broadcast_to(primal_values, (8, count)), hot_coarse, NT)[0:1]
-    copies_d = send_all(coarse_send, coarse_in, d_send, d_recv)
+    send_all(coarse_send, coarse_in, d_send, d_recv)
     finish(
         [
             group_copy(
@@ -636,8 +647,8 @@
     lax.fori_loop(0, mult_rows // 8, image_step, 0)
 
     inputs["inverse"].wait()
-    finish(copies_d)
-    coarse = sum(coarse_in[d] for d in range(groups * pencils))
+    finish_all(coarse_send, coarse_in, d_send, d_recv)
+    coarse = jnp.sum(coarse_in[...], axis=0)
     lifted = split_dot(jnp.broadcast_to(coarse, (8, coarse_count)), inverse_ref[...], NT)
     lifts = hot_dot(lifted, hot_meets[...])[0:1]
     jump_lift = hot_dot(meet_rows[...] * lifts, meet_lanes[...], NT)
@@ -658,8 +669,9 @@
     ]
     lane = iota((1, LANES), 1)
     sums_send[...] = sum(jnp.where(lane == n, value, 0.0) for n, value in enumerate(parts))
-    finish(send_all(sums_send, sums_in, f_send, f_recv))
-    sums = sum(sums_in[d] for d in range(groups * pencils))
+    send_all(sums_send, sums_in, f_send, f_recv)
+    finish_all(sums_send, sums_in, f_send, f_recv)
+    sums = jnp.sum(sums_in[...], axis=0)
     totals = [sums[:, n : n + 1] for n in range(4)]
     old, curvature = totals[0], totals[1]
     alpha = old / curvature

time: 49.8 us -> 50.1 us (level)
  no operation moved by 1% of the time
where the time goes in v5:
time: 50.1 us; the launch traced here: 49.9 us
  Pallas kernels  47.6 us (95%)
  other arithmetic  1.61 us (3%)
  between operations  0.64 us (1%)
    pallas_call x1, Pallas kernels, body(): pl.pallas_call(functools.partial(kernel, groups, pencils), out_shape=[jax...  47.6 us
    add x1, other arithmetic, body(): next_dir = mult_scale * next_resid + beta * direction  1.61 us

profile of v5, /device:TPU:0, one launch (start us, length us, event | category | flops | bytes accessed | tf_op | source)
XLA Modules:
  0.0 49.9 jit_solution(1003778830160214311)
XLA Ops:
  0.6 47.6 %tearing_step.1 = (f32[64,128]{1,0:T(8,128)}, f32[64,128]{1,0:T(8,128)}, f32[64,128]{1,0:T(8,128)}) custom-call(f32[64,128]{1,0:T(8,128)} %bitcast.12, f32[64,128]{1,0:T(8,128)} %bitcast.13, f32[64,128]{1,0:T(8,128)} %bitcast.14, f32[4,3,64,64]{3,2,1,0:T(8,128)} %basis_hbm.1, f32[3,4,64]{2,1,0:T(4,128)} %bitcast.20, f32[3,4,3]{2,1,0:T(4,128)} %bitcast.21, ...), custom_call_target="tpu_custom_call" | custom-call | tf_op jit(solution)/shard_map/tearing_step/pallas_call | solution.py:791
  48.3 1.6 %multiply_add_fusion = (f32[1,1,8192]{2,1,0:T(1,128)}, f32[1,1,8192]{2,1,0:T(1,128)}, f32[1,1,8192]{2,1,0:T(1,128)}) fusion(f32[1,1,8192]{2,1,0:T(1,128)} %bitcast.19, f32[1,1,8192]{2,1,0:T(1,128)} %param.14, f32[1,1,8192]{2,1,0:T(1,128)} %param.15, f32[1,1,8192]{2,1,0:T(1,128)} %param.13, f32[1,1,8192]{2,1,0:T(1,128)} %bitcast.18, f32[1,1,8192]{2,1,0:T(1,128)} %bitcast.17, ...), kind=kLoop, calls=%fused_computation | loop fusion | flops 57344 | bytes 327680 | tf_op jit(solution)/shard_map/add | solution.py:817

commit v6 on v5

--- a/solution.py
+++ b/solution.py
@@ -228,7 +228,7 @@
         return copies
 
     def device_peer(number):
-        return group_peer(number // pencils), pencil_peer(lax.rem(number, pencils))
+        return group_peer(number // pencils), pencil_peer(number % pencils)
 
     def all_copy(src, landing, send, recv, number):
         return pltpu.make_async_remote_copy(
@@ -241,11 +241,8 @@
         )
 
     def each_device(action):
-        def step(number, carry):
+        for number in range(1, groups * pencils):
             action(number)
-            return carry
-
-        lax.fori_loop(1, groups * pencils, step, 0)
 
     def send_all(src, landing, send, recv):
         each_device(lambda number: all_copy(src, landing, send, recv, number).start())
@@ -562,8 +559,8 @@
         for u in range(1, dup):
             total = total + out_in[p * dup + u]
         top, rest_part = halves(total)
-        table[p * chunk : (p + 1) * chunk, 0:slots] = top
-        table[p * chunk : (p + 1) * chunk, slots : 2 * slots] = rest_part
+        table[p * chunk : (p + 1) * chunk, :] = top
+        table[table_rows + p * chunk : table_rows + (p + 1) * chunk, :] = rest_part
     lookup = table[...].astype(BF16)
     places = iota((table_rows, LANES), 0).astype(F32)
 
@@ -579,7 +576,8 @@
                 ],
                 axis=1,
             )
-            both = fast_dot(lookup, jnp.concatenate([hot, hot], axis=0))
+            both = fast_dot(lookup, hot)
+            both = both[0:table_rows] + both[table_rows : 2 * table_rows]
             for u in range(2):
                 here = places == rows[i + u : i + u + 1]
                 found.append(
@@ -744,7 +742,7 @@
         vmem(slots, width),
         vmem(pencils, chunk, slots),
         vmem(pencils, chunk, slots),
-        vmem(table_rows, 2 * slots),
+        vmem(2 * table_rows, slots),
         vmem(*share),
         vmem(1, coarse_count),
         vmem(devices, 1, coarse_count),

time: 50.1 us -> 49.4 us (0.986)
  Pallas kernels: 47.6 us -> 46.9 us
    pallas_call x1, Pallas kernels: 47.6 us -> 46.9 us  [body(): pl.pallas_call(functools.partial(kernel, groups, pencils), out_shape=[jax...]
where the time goes in v6:
time: 49.4 us; the launch traced here: 49.2 us
  Pallas kernels  46.9 us (95%)
  other arithmetic  1.61 us (3%)
  between operations  0.64 us (1%)
    pallas_call x1, Pallas kernels, body(): pl.pallas_call(functools.partial(kernel, groups, pencils), out_shape=[jax...  46.9 us
    add x1, other arithmetic, body(): next_dir = mult_scale * next_resid + beta * direction  1.61 us

profile of v6, /device:TPU:0, one launch (start us, length us, event | category | flops | bytes accessed | tf_op | source)
XLA Modules:
  0.0 49.2 jit_solution(11234668440661660368)
XLA Ops:
  0.6 46.9 %tearing_step.1 = (f32[64,128]{1,0:T(8,128)}, f32[64,128]{1,0:T(8,128)}, f32[64,128]{1,0:T(8,128)}) custom-call(f32[64,128]{1,0:T(8,128)} %bitcast.12, f32[64,128]{1,0:T(8,128)} %bitcast.13, f32[64,128]{1,0:T(8,128)} %bitcast.14, f32[4,3,64,64]{3,2,1,0:T(8,128)} %basis_hbm.1, f32[3,4,64]{2,1,0:T(4,128)} %bitcast.20, f32[3,4,3]{2,1,0:T(4,128)} %bitcast.21, ...), custom_call_target="tpu_custom_call" | custom-call | tf_op jit(solution)/shard_map/tearing_step/pallas_call | solution.py:789
  47.5 1.6 %multiply_add_fusion = (f32[1,1,8192]{2,1,0:T(1,128)}, f32[1,1,8192]{2,1,0:T(1,128)}, f32[1,1,8192]{2,1,0:T(1,128)}) fusion(f32[1,1,8192]{2,1,0:T(1,128)} %bitcast.19, f32[1,1,8192]{2,1,0:T(1,128)} %param.14, f32[1,1,8192]{2,1,0:T(1,128)} %param.15, f32[1,1,8192]{2,1,0:T(1,128)} %param.13, f32[1,1,8192]{2,1,0:T(1,128)} %bitcast.18, f32[1,1,8192]{2,1,0:T(1,128)} %bitcast.17, ...), kind=kLoop, calls=%fused_computation | loop fusion | flops 57344 | bytes 327680 | tf_op jit(solution)/shard_map/add | solution.py:815
